TPU v7x, 512 devices: a whole 4x8x8 slice. The times are simulated.
512 devices in a mesh: replica: 64 (over z_lo, y, core), tensor: 8 (over z_hi, x).
Axes of the slice: x: 4, y: 8, z: 8 (z_hi: 2, z_lo: 4; z = z_hi * 4 + z_lo), core: 2. Of those that a mesh axis runs over, the one named last changes fastest.
Arguments:
- owner: int32 [192], replicated, may hold values from 0 to 63, as said below
- qkv: bfloat16 [3, 384, 64, 2048], P(None, 'replica', None, 'tensor'), may hold values from -6 to 6
- grad_out: bfloat16 [192, 64, 3200], P('replica', 'tensor'), may hold values from -1.5 to 1.5
- w_out: bfloat16 [128, 16, 3200], P(None, 'tensor'), may hold values from -0.125 to 0.125
- layer_scale: float32 [3200], replicated, may hold values from 0.1 to 1.9
Outputs:
- grad_qkv: bfloat16 [3, 384, 64, 2048], P(None, 'replica', None, 'tensor')
- grad_w: float32 [128, 16, 3200], P('replica', 'tensor')
- grad_scale: float32 [3200], replicated
Inputs may be any that keep to these rules, and one draw needn't show every extreme that they name: `owner`: image i comes from source device i // 3. At most 2 images of one source device go to one replica, and some source sends exactly 2 to one replica. A replica works on at most 6 images, some on exactly 6; every replica's count is a multiple of 3.
All inputs are finite; a program needn't handle non-finite values.
Results may differ from a plain program's by a relative error of at most 0.02.
Values may be sent and summed in bfloat16 or wider, within the bound.
No kernel may reach another device: no remote copies, remote signals or barrier semaphores. Data moves between devices by JAX's collectives and lax.ppermute only.
A program may use at most 64 MiB of HBM per device.

v0:
```python
import jax
import jax.numpy as jnp
from jax import lax
from jax.sharding import PartitionSpec as P


def attention_backward(queries, keys_in, values, dealt, weights, layer_scale, head_size):
    factor = head_size ** (-0.5)
    scores = (
        jnp.einsum("mqhe,mkhe->mhqk", queries, keys_in, preferred_element_type=jnp.float32) * factor
    )
    row_peak = jnp.max(scores, axis=-1, keepdims=True)
    raised = jnp.exp(scores - row_peak)
    probs = raised / jnp.sum(raised, axis=-1, keepdims=True)
    probs_low = probs.astype(jnp.bfloat16)
    attended = jnp.einsum(
        "mhqk,mkhe->mqhe", probs_low, values, preferred_element_type=jnp.float32
    ).astype(jnp.bfloat16)
    scaled = (dealt.astype(jnp.float32) * layer_scale).astype(jnp.bfloat16)
    d_attended = jnp.einsum(
        "mtc,ehc->mthe", scaled, weights, preferred_element_type=jnp.float32
    ).astype(jnp.bfloat16)
    d_values = jnp.einsum(
        "mhqk,mqhe->mkhe", probs_low, d_attended, preferred_element_type=jnp.float32
    ).astype(jnp.bfloat16)
    d_probs = jnp.einsum("mqhe,mkhe->mhqk", d_attended, values, preferred_element_type=jnp.float32)
    row_total = jnp.sum(probs * d_probs, axis=-1, keepdims=True)
    d_scores = (probs * (d_probs - row_total) * factor).astype(jnp.bfloat16)
    d_query = jnp.einsum(
        "mhqk,mkhe->mqhe", d_scores, keys_in, preferred_element_type=jnp.float32
    ).astype(jnp.bfloat16)
    d_keys = jnp.einsum(
        "mhqk,mqhe->mkhe", d_scores, queries, preferred_element_type=jnp.float32
    ).astype(jnp.bfloat16)
    return (jnp.stack([d_query, d_keys, d_values]), attended, scaled)


def local(owner, qkv, grad_out, w_out, layer_scale):
    slot_count = qkv.shape[1]
    head_size = w_out.shape[0]
    local_heads = w_out.shape[1]
    receiver = lax.axis_index("replica")
    mine = owner == receiver
    mine_int = mine.astype(jnp.int32)
    slot_of = jnp.cumsum(mine_int) - mine_int
    slot_ids = jnp.arange(slot_count, dtype=jnp.int32)
    selector = ((slot_of[None, :] == slot_ids[:, None]) & (mine_int[None, :] == 1)).astype(
        jnp.bfloat16
    )
    moved = jnp.einsum(
        "mi,itc->mtc",
        selector,
        lax.all_gather(grad_out, "replica", axis=0, tiled=True),
        preferred_element_type=jnp.float32,
    )
    compact = moved.astype(jnp.bfloat16)
    dealt = lax.all_gather(compact, "tensor", axis=1, tiled=True)
    tokens = dealt.shape[1]
    block = qkv.reshape(3, slot_count, tokens, local_heads, head_size)
    grads, attended, scaled = attention_backward(
        block[0], block[1], block[2], dealt, w_out, layer_scale, head_size
    )
    grad_qkv = grads.reshape(3, slot_count, tokens, local_heads * head_size)
    grad_w = lax.psum_scatter(
        jnp.einsum("mthe,mtc->ehc", attended, scaled, preferred_element_type=jnp.float32),
        "replica",
        scatter_dimension=0,
        tiled=True,
    )
    projected = jnp.einsum("mthe,ehc->mtc", attended, w_out, preferred_element_type=jnp.float32)
    scale_part = jnp.sum(dealt.astype(jnp.float32) * projected, axis=(0, 1))
    grad_scale = lax.psum(scale_part, ("replica", "tensor"))
    return (grad_qkv, grad_w, grad_scale)


def solution(mesh):
    in_specs = (
        P(),
        P(None, "replica", None, "tensor"),
        P("replica", "tensor", None),
        P(None, "tensor", None),
        P(),
    )
    out_specs = (P(None, "replica", None, "tensor"), P("replica", "tensor", None), P())
    return jax.shard_map(local, mesh=mesh, in_specs=in_specs, out_specs=out_specs, check_vma=False)
```

profile of v0, /device:TPU:2, one launch (start us, length us, event | category | flops | bytes accessed | tf_op | source)
XLA Modules:
  0.0 784.2 jit_solution(10309588656816487871)
XLA Ops:
  7.2 0.7 all-gather.3.cloned.1.call-update
  7.9 0.7 broadcast_compare_fusion
  8.6 0.3 reduce-window.9
  9.3 132.6 %all-gather.3.cloned.1.call-done = bf16[192,8,3200]{2,1,0:T(8,128)(2,1)} async-done(((bf16[3,8,3200]{2,1,0:T(8,128)(2,1)}), bf16[192,8,3200]{2,1,0:T(8,128)(2,1)}) %all-gather.3.cloned.1.call-update) | async-done | bytes 9830416 | tf_op jit(solution)/shard_map/all_gather | solution.py:53
  141.8 6.4 fusion.5
  148.3 0.7 copy.40
  149.3 1.0 fusion.88
  150.4 1.1 fusion.30
  151.5 82.5 %all-gather.5.cloned.1.call-done = bf16[6,64,3200]{2,1,0:T(8,128)(2,1)} async-done(((bf16[6,8,3200]{2,1,0:T(8,128)(2,1)}), bf16[6,64,3200]{2,1,0:T(8,128)(2,1)}) %all-gather.5.cloned.1.call-update) | async-done | bytes 2457616 | tf_op jit(solution)/shard_map/all_gather | solution.py:57
  234.0 2.7 convolution_bitcast_fusion.1
  236.8 4.3 copy.52
  241.1 1.4 dynamic-slice
  243.2 2.3 fusion.32
  245.6 0.2 fusion.44
  245.8 1.5 fusion.28
  247.3 0.2 copy.45
  247.7 1.5 fusion.29
  249.2 0.2 copy.47
  249.5 0.4 fusion.31
  250.3 2.6 fusion.9
  252.9 97.3 %psum.7 = f32[3200]{0:T(1024)} all-reduce(f32[3200]{0:T(1024)S(1)} %fusion.9), channel_id=1, replica_groups=mesh['replica'=64,'tensor'=8] {'replica','tensor'}, use_global_device_ids=true, to_apply=%region_7.8 | all-reduce | flops 3200 | bytes 25600 | tf_op jit(solution)/shard_map/psum | solution.py:72
  350.2 0.9 pad_maximum_fusion
  351.1 425.1 %all-reduce.4.cloned.1.call-done = f32[128,2,3200]{2,1,0:T(2,128)} async-done(((f32[128,2,3200]{2,1,0:T(2,128)}), f32[128,2,3200]{2,1,0:T(2,128)}) %all-reduce.4.cloned.1.call-update) | async-done | bytes 3276816
  776.2 1.4 constant_dynamic-slice_fusion
  (37 shorter events, 1.3 us)
Async XLA Ops:
  7.2 134.7 %all-gather.3.cloned.1.call-start = ((), (), s32[]{:S(2)}) async-start(), calls=%async_computation | async-start | bytes 9984000 | tf_op jit(solution)/shard_map/all_gather | solution.py:53
  7.9 226.1 %all-gather.5.cloned.1.call-start = ((), (), s32[]{:S(2)}) async-start(), calls=%async_computation.1 | async-start | bytes 2764800 | tf_op jit(solution)/shard_map/all_gather | solution.py:57
  141.8 7.2 copy-start
  148.3 85.8 %copy-start.7 = (f32[3200]{0:T(1024)S(1)}, f32[3200]{0:T(1024)}, u32[]{:S(2)}) copy-start(f32[3200]{0:T(1024)} %param.9) | copy-start | bytes 38404
  149.0 627.2 %all-reduce.4.cloned.1.call-start = ((), (), s32[]{:S(2)}) async-start(), calls=%async_computation.2 | async-start | bytes 6553600
  149.3 2.2 copy-start.1
  149.3 2.2 copy-start.3
  241.1 2.1 copy-start.5
  243.2 2.6 copy-start.2
  245.6 2.1 copy-start.4
  247.5 2.8 copy-start.6
  247.5 2.8 copy-start.8
Sparse Core Ops, SparseCore 0:
  10.2 131.6 all-gather.2
  149.1 84.8 all-gather.4
  241.2 534.9 all-reduce.3
where the time goes:
time: 785 us; the launch traced here: 784 us
  waiting for transfers between devices  641 us (82%)
  blocking collectives  97.3 us (12%)
  matrix products  19.8 us (3%)
  between operations  14.6 us (2%)
  local copies, waits for them, and re-layouts  9.34 us (1%)
    unnamed x4, waiting for transfers between devices  426 us
    all_gather x1, waiting for transfers between devices, local(): lax.all_gather(grad_out, 'replica', axis=0, tiled=True)  133 us
    psum x1, blocking collectives, local(): grad_scale = lax.psum(scale_part, ('replica', 'tensor'))  97.3 us
    all_gather x1, waiting for transfers between devices, local(): dealt = lax.all_gather(compact, 'tensor', axis=1, tiled=True)  82.5 us
  transfers between devices with their start and end apart: 3, of which 3 were waited for; matrix products, arithmetic and copies ran while one was open for 2% of the time, Pallas kernels for 0%

commit v1 on v0

v1 whole, which is shorter than its diff:
```python
import jax
import jax.numpy as jnp
from jax import lax
from jax.sharding import PartitionSpec as P

N_X = 4


def tensor_step(shift_hi, shift_x):
    pairs = []
    for index in range(8):
        high, x = index // N_X, index % N_X
        pairs.append((index, (high + shift_hi) % 2 * N_X + (x + shift_x) % N_X))
    return pairs


def deal(owner, grad_out, slot_count):
    replicas, runs = 64, 5
    images, tokens, width = grad_out.shape
    ids = jnp.arange(replicas * images, dtype=jnp.int32)
    same = (owner[:, None] == owner[None, :]) & (ids[None, :] < ids[:, None])
    slot_of = owner * slot_count + jnp.sum(same.astype(jnp.int32), axis=1)
    slots = jnp.arange(replicas * slot_count, dtype=jnp.int32)
    chosen = (slots[:, None] == slot_of[None, :]).astype(grad_out.dtype)

    pieces = grad_out.reshape(images, tokens, runs, width // runs).transpose(1, 2, 0, 3)
    pieces = pieces.reshape(tokens * runs, images, width // runs)
    pieces = jnp.pad(pieces, ((0, replicas - tokens * runs), (0, 0), (0, 0)))
    held = lax.all_to_all(pieces, "replica", 0, 0).reshape(replicas * images, width // runs)
    dealt = jnp.einsum("mi,ic->mc", chosen, held, preferred_element_type=jnp.float32)
    dealt = dealt.astype(grad_out.dtype).reshape(replicas, slot_count, width // runs)
    mine = lax.all_to_all(dealt, "replica", 0, 0)[: tokens * runs]
    mine = mine.reshape(tokens, runs, slot_count, width // runs).transpose(2, 0, 1, 3)
    return mine.reshape(slot_count, tokens, width)


def ring_gather(block):
    half = block.shape[0] // 2
    ahead, behind = tensor_step(0, 1), tensor_step(0, -1)
    from_left = lax.ppermute(block, "tensor", ahead)
    from_right = lax.ppermute(block, "tensor", behind)
    far_low = lax.ppermute(from_left[:half], "tensor", ahead)
    far_high = lax.ppermute(from_right[half:], "tensor", behind)
    return [block, from_left, from_right, jnp.concatenate([far_low, far_high])]


def gather_tokens(block):
    other = lax.ppermute(block, "tensor", tensor_step(1, 0))
    near = ring_gather(block)
    far = ring_gather(other)
    me = lax.axis_index("tensor")
    high, x = me // N_X, me % N_X
    places = []
    for hi in (high, 1 - high):
        for step in (0, -1, 1, 2):
            places.append(hi * N_X + (x + step + N_X) % N_X)
    return jnp.stack(near + far), jnp.stack(places)


def local(owner, qkv, grad_out, w_out, layer_scale):
    slots, tokens = qkv.shape[1], qkv.shape[2]
    size, heads, width = w_out.shape
    groups = 8
    run = tokens // groups
    factor = size ** (-0.5)

    dealt = deal(owner, grad_out, slots)

    block = qkv.reshape(3, slots, tokens, heads, size)
    queries, keys_in, values = block[0], block[1], block[2]
    scores = (
        jnp.einsum("mqhe,mkhe->mhqk", queries, keys_in, preferred_element_type=jnp.float32) * factor
    )
    raised = jnp.exp(scores - jnp.max(scores, axis=-1, keepdims=True))
    probs = raised / jnp.sum(raised, axis=-1, keepdims=True)
    probs_low = probs.astype(jnp.bfloat16)
    attended = jnp.einsum(
        "mhqk,mkhe->mqeh", probs_low, values, preferred_element_type=jnp.float32
    ).astype(jnp.bfloat16)
    weights = w_out.reshape(size * heads, width)
    scaled_weights = (weights.astype(jnp.float32) * layer_scale).astype(jnp.bfloat16)

    pieces, places = gather_tokens(dealt)
    grouped = attended.reshape(slots, groups, run, size * heads).transpose(1, 0, 2, 3)
    in_order = grouped[places].reshape(groups * slots * run, size * heads)
    flat = pieces.reshape(groups * slots * run, width)
    product = jnp.einsum("nw,nc->wc", in_order, flat, preferred_element_type=jnp.float32)
    partial = (product * layer_scale).astype(jnp.bfloat16)
    scale_part = jnp.sum(product * weights.astype(jnp.float32), axis=0).astype(jnp.bfloat16)

    replicas = 64
    rows = size * heads // replicas
    outgoing = jnp.concatenate(
        [
            partial.reshape(replicas, rows, width),
            jnp.broadcast_to(scale_part, (replicas, 1, width)),
        ],
        axis=1,
    )
    arrived = lax.all_to_all(outgoing, "replica", 0, 0)
    summed = jnp.sum(arrived.astype(jnp.float32), axis=0)
    grad_w = summed[:rows].reshape(size // replicas, heads, width)
    scale_copies = jnp.broadcast_to(summed[rows], (groups, width))
    grad_scale = jnp.sum(lax.all_to_all(scale_copies, "tensor", 0, 0), axis=0)

    d_flat = jnp.einsum(
        "nc,wc->nw", flat, scaled_weights, preferred_element_type=jnp.float32
    ).astype(jnp.bfloat16)
    d_grouped = d_flat.reshape(groups, slots, run, size, heads)
    back = jnp.argsort(places)
    d_attended = d_grouped[back].transpose(1, 0, 2, 4, 3).reshape(slots, tokens, heads, size)
    d_values = jnp.einsum(
        "mhqk,mqhe->mkhe", probs_low, d_attended, preferred_element_type=jnp.float32
    ).astype(jnp.bfloat16)
    d_probs = jnp.einsum("mqhe,mkhe->mhqk", d_attended, values, preferred_element_type=jnp.float32)
    row_total = jnp.sum(probs * d_probs, axis=-1, keepdims=True)
    d_scores = (probs * (d_probs - row_total) * factor).astype(jnp.bfloat16)
    d_query = jnp.einsum(
        "mhqk,mkhe->mqhe", d_scores, keys_in, preferred_element_type=jnp.float32
    ).astype(jnp.bfloat16)
    d_keys = jnp.einsum(
        "mhqk,mqhe->mkhe", d_scores, queries, preferred_element_type=jnp.float32
    ).astype(jnp.bfloat16)
    grad_qkv = jnp.stack([d_query, d_keys, d_values]).reshape(3, slots, tokens, heads * size)
    return (grad_qkv, grad_w, grad_scale)


def solution(mesh):
    in_specs = (
        P(),
        P(None, "replica", None, "tensor"),
        P("replica", "tensor", None),
        P(None, "tensor", None),
        P(),
    )
    out_specs = (P(None, "replica", None, "tensor"), P("replica", "tensor", None), P())
    return jax.shard_map(local, mesh=mesh, in_specs=in_specs, out_specs=out_specs, check_vma=False)
```

time: 785 us -> 224 us (0.29)
  the two profiles are of different devices: /device:TPU:2 before, /device:TPU:24 now
where the time goes in v1:
time: 224 us; the launch traced here: 223 us
  starting transfers between devices  79.8 us (36%)
  waiting for transfers between devices  73 us (33%)
  local copies, waits for them, and re-layouts  40.8 us (18%)
  matrix products  15.8 us (7%)
  other arithmetic  12.2 us (5%)
    all_to_all x1, waiting for transfers between devices, local(): arrived = lax.all_to_all(outgoing, 'replica', 0, 0)  41.1 us
    all_to_all x1, starting transfers between devices, deal(): lax.all_to_all(pieces, 'replica', 0, 0)  13.3 us
    all_to_all x1, starting transfers between devices, local(): arrived = lax.all_to_all(outgoing, 'replica', 0, 0)  12.6 us
    all_to_all x1, waiting for transfers between devices, deal(): lax.all_to_all(pieces, 'replica', 0, 0)  10.3 us
    ppermute x2, starting transfers between devices, ring_gather(): far_high = lax.ppermute(from_right[half:], 'tensor', behind)  10.3 us
    all_to_all x1, starting transfers between devices, local(): grad_scale = jnp.sum(lax.all_to_all(scale_copies, 'tensor', 0, 0), axis=0)  9.88 us
    ppermute x2, starting transfers between devices, ring_gather(): from_right = lax.ppermute(block, 'tensor', behind)  8.52 us
    ppermute x1, starting transfers between devices, gather_tokens(): other = lax.ppermute(block, 'tensor', tensor_step(1, 0))  8.22 us
  transfers between devices with their start and end apart: 13, of which 8 were waited for; matrix products, arithmetic and copies ran while one was open for 24% of the time, Pallas kernels for 0%

profile of v1, /device:TPU:24, one launch (start us, length us, event | category | flops | bytes accessed | tf_op | source)
XLA Modules:
  0.0 222.9 jit_solution(7152813873992968536)
XLA Ops:
  2.5 13.3 %all-to-all-start = ((bf16[64,3,640]{2,1,0:T(4,128)(2,1)}), bf16[64,3,640]{2,1,0:T(4,128)(2,1)S(1)}, u32[]{:S(2)}, u32[]{:S(2)}) async-start(bf16[64,3,640]{2,1,0:T(4,128)(2,1)} %pad.4.clone), calls=%async_computation | async-start | bytes 655360 | tf_op jit(solution)/shard_map/all_to_all | solution.py:29
  17.5 10.3 %all-to-all-done = bf16[64,3,640]{2,1,0:T(4,128)(2,1)S(1)} async-done(((bf16[64,3,640]{2,1,0:T(4,128)(2,1)}), bf16[64,3,640]{2,1,0:T(4,128)(2,1)S(1)}, u32[]{:S(2)}, u32[]{:S(2)}) %all-to-all-start) | async-done | bytes 245792 | tf_op jit(solution)/shard_map/all_to_all | solution.py:29
  29.4 7.3 %all-to-all-start.1 = ((bf16[64,6,640]{2,1,0:T(8,128)(2,1)}), bf16[64,6,640]{2,1,0:T(8,128)(2,1)}, u32[]{:S(2)}, u32[]{:S(2)}) async-start(bf16[64,6,640]{2,1,0:T(8,128)(2,1)} %reshape.395), calls=%async_computation.1 | async-start | bytes 1310720 | tf_op jit(solution)/shard_map/all_to_all | solution.py:32
  42.9 3.6 %reshape.404 = f32[256,3200]{1,0:T(8,128)S(1)} reshape(bf16[128,2,3200]{2,1,0:T(2,128)(2,1)} %param.8) | data formatting | bytes 4915200 | tf_op jit(solution)/shard_map/convert_element_type | solution.py:81
  47.9 7.1 %all-to-all-done.1 = bf16[64,6,640]{2,1,0:T(8,128)(2,1)} async-done(((bf16[64,6,640]{2,1,0:T(8,128)(2,1)}), bf16[64,6,640]{2,1,0:T(8,128)(2,1)}, u32[]{:S(2)}, u32[]{:S(2)}) %all-to-all-start.1) | async-done | bytes 491552 | tf_op jit(solution)/shard_map/all_to_all | solution.py:32
  56.0 3.4 %collective-permute-start = (bf16[6,8,3200]{2,1,0:T(8,128)(2,1)S(1)}, bf16[6,8,3200]{2,1,0:T(8,128)(2,1)S(1)}, u32[]{:S(2)}, u32[]{:S(2)}) collective-permute-start(bf16[6,8,3200]{2,1,0:T(8,128)(2,1)S(1)} %bitcast.84), channel_id=1, source_target_pairs={{0,1},{1,2},{2,3},{3,0},{4,5},{5,6},{6,7},{7,4},{8,9},{9,10},{10,1... | collective-permute-start | bytes 921608 | tf_op jit(solution)/shard_map/ppermute | solution.py:40
  59.5 3.7 %collective-permute-start.1 = (bf16[6,8,3200]{2,1,0:T(8,128)(2,1)S(1)}, bf16[6,8,3200]{2,1,0:T(8,128)(2,1)S(1)}, u32[]{:S(2)}, u32[]{:S(2)}) collective-permute-start(bf16[6,8,3200]{2,1,0:T(8,128)(2,1)S(1)} %bitcast.85), channel_id=1, source_target_pairs={{0,3},{1,0},{2,1},{3,2},{4,7},{5,4},{6,5},{7,6},{8,11},{9,8},{10,9... | collective-permute-start | bytes 921608 | tf_op jit(solution)/shard_map/ppermute | solution.py:41
  63.1 8.2 %collective-permute-start.4 = (bf16[6,8,3200]{2,1,0:T(8,128)(2,1)S(1)}, bf16[6,8,3200]{2,1,0:T(8,128)(2,1)S(1)}, u32[]{:S(2)}, u32[]{:S(2)}) collective-permute-start(bf16[6,8,3200]{2,1,0:T(8,128)(2,1)S(1)} %bitcast.86), channel_id=1, source_target_pairs={{0,4},{1,5},{2,6},{3,7},{4,0},{5,1},{6,2},{7,3},{8,12},{9,13},{10,... | collective-permute-start | bytes 921608 | tf_op jit(solution)/shard_map/ppermute | solution.py:48
  73.7 5.0 %collective-permute-start.3 = (bf16[3,8,3200]{2,1,0:T(8,128)(2,1)S(1)}, bf16[3,8,3200]{2,1,0:T(8,128)(2,1)S(1)}, u32[]{:S(2)}, u32[]{:S(2)}) collective-permute-start(bf16[3,8,3200]{2,1,0:T(8,128)(2,1)S(1)} %slice.52), channel_id=1, source_target_pairs={{0,3},{1,0},{2,1},{3,2},{4,7},{5,4},{6,5},{7,6},{8,11},{9,8},{10,9... | collective-permute-start | bytes 460808 | tf_op jit(solution)/shard_map/ppermute | solution.py:43
  82.5 4.9 %collective-permute-start.6 = (bf16[6,8,3200]{2,1,0:T(8,128)(2,1)S(1)}, bf16[6,8,3200]{2,1,0:T(8,128)(2,1)S(1)}, u32[]{:S(2)}, u32[]{:S(2)}) collective-permute-start(bf16[6,8,3200]{2,1,0:T(8,128)(2,1)S(1)} %collective-permute-done.4), channel_id=1, source_target_pairs={{0,3},{1,0},{2,1},{3,2},{4,7},{5,4},{6,5},{7,6},{8,11},{9,8},{10,9... | collective-permute-start | bytes 921608 | tf_op jit(solution)/shard_map/ppermute | solution.py:41
  87.5 4.4 %collective-permute-done.5 = bf16[6,8,3200]{2,1,0:T(8,128)(2,1)S(1)} collective-permute-done((bf16[6,8,3200]{2,1,0:T(8,128)(2,1)S(1)}, bf16[6,8,3200]{2,1,0:T(8,128)(2,1)S(1)}, u32[]{:S(2)}, u32[]{:S(2)}) %collective-permute-start.5) | collective-permute-done | bytes 307232 | tf_op jit(solution)/shard_map/ppermute | solution.py:40
  93.9 5.3 %collective-permute-start.8 = (bf16[3,8,3200]{2,1,0:T(8,128)(2,1)S(1)}, bf16[3,8,3200]{2,1,0:T(8,128)(2,1)S(1)}, u32[]{:S(2)}, u32[]{:S(2)}) collective-permute-start(bf16[3,8,3200]{2,1,0:T(8,128)(2,1)S(1)} %slice.54), channel_id=1, source_target_pairs={{0,3},{1,0},{2,1},{3,2},{4,7},{5,4},{6,5},{7,6},{8,11},{9,8},{10,9... | collective-permute-start | bytes 460808 | tf_op jit(solution)/shard_map/ppermute | solution.py:43
  104.1 2.9 %reshape.402 = bf16[64,4,3200]{2,1,0:T(4,128)(2,1)S(1)} reshape(bf16[256,3200]{1,0:T(8,128)(2,1)} %get-tuple-element.5) | data formatting | bytes 3276800 | tf_op jit(solution)/shard_map/reshape | solution.py:95
  107.5 3.4 %pad_maximum_fusion = bf16[64,5,3200]{2,1,0:T(8,128)(2,1)} fusion(bf16[64,1,3200]{2,1,0:T(2,128)(2,1)S(1)} %broadcast_in_dim.7, bf16[64,4,3200]{2,1,0:T(4,128)(2,1)S(1)} %reshape.402), kind=kLoop, calls=%fused_computation.6 | loop fusion | flops 4096000 | bytes 4096000 | tf_op jit(solution)/shard_map/concatenate | solution.py:93
  110.9 12.6 %all-to-all-start.2 = ((bf16[64,5,3200]{2,1,0:T(8,128)(2,1)}), bf16[64,5,3200]{2,1,0:T(8,128)(2,1)S(1)}, u32[]{:S(2)}, u32[]{:S(2)}) async-start(bf16[64,5,3200]{2,1,0:T(8,128)(2,1)} %pad_maximum_fusion), calls=%async_computation.2 | async-start | bytes 6553600 | tf_op jit(solution)/shard_map/all_to_all | solution.py:100
  123.5 3.9 %multiply_convert_fusion.1 = bf16[128,2,3200]{2,1,0:T(2,128)(2,1)} fusion(f32[3200]{0:T(1024)S(1)} %copy-done.8, bf16[128,2,3200]{2,1,0:T(2,128)(2,1)} %param.8), kind=kLoop, calls=%fused_computation.9 | loop fusion | flops 2457600 | bytes 3289600 | tf_op jit(solution)/shard_map/convert_element_type | solution.py:81
  127.4 4.7 %convert_element_type.71 = bf16[256,3200]{1,0:T(8,128)(2,1)} reshape(bf16[128,2,3200]{2,1,0:T(2,128)(2,1)} %multiply_convert_fusion.1) | data formatting | bytes 3276800 | tf_op jit(solution)/shard_map/convert_element_type | solution.py:81
  133.2 3.7 %convolution_convert_fusion.1 = bf16[384,256]{1,0:T(8,128)(2,1)} fusion(bf16[384,3200]{1,0:T(8,128)(2,1)} %bitcast.91, bf16[256,3200]{1,0:T(8,128)(2,1)} %convert_element_type.71), kind=kOutput, calls=%fused_computation.17 | convolution fusion | flops 629243904 | bytes 4292608 | tf_op jit(solution)/shard_map/nc,wc->nw/dot_general | solution.py:106
  138.0 5.0 %reshape.399 = bf16[8,6,8,128,2]{2,1,0,4,3:T(8,128)(2,1)} reshape(bf16[384,256]{0,1:T(8,128)(2,1)S(1)} %copy.88) | data formatting | bytes 393216 | tf_op jit(solution)/shard_map/reshape | solution.py:109
  143.0 6.0 %gather_fusion = bf16[8,6,8,128,2]{2,1,4,3,0:T(8,128)(2,1)} fusion(bf16[8,6,8,128,2]{2,1,0,4,3:T(8,128)(2,1)} %reshape.399, s32[1024]{0:T(1024)S(1)} %pad_clamp_fusion.1), kind=kCustom, calls=%fused_computation | custom fusion | bytes 393248 | tf_op jit(solution)/shard_map/gather | solution.py:111
  149.0 4.1 %copy.89 = bf16[6,8,8,2,128]{4,2,1,3,0:T(8,128)(2,1)S(1)} copy(bf16[6,8,8,2,128]{2,0,3,4,1:T(8,128)(2,1)} %bitcast.82) | data formatting | bytes 393216 | tf_op jit(solution)/shard_map/transpose | solution.py:111
  159.5 41.1 %all-to-all-done.2 = bf16[64,5,3200]{2,1,0:T(8,128)(2,1)S(1)} async-done(((bf16[64,5,3200]{2,1,0:T(8,128)(2,1)}), bf16[64,5,3200]{2,1,0:T(8,128)(2,1)S(1)}, u32[]{:S(2)}, u32[]{:S(2)}) %all-to-all-start.2) | async-done | bytes 2048032 | tf_op jit(solution)/shard_map/all_to_all | solution.py:100
  202.0 9.9 %all-to-all-start.3 = ((f32[8,1,3200]{2,1,0:T(1,128)}), f32[8,1,3200]{2,1,0:T(1,128)S(1)}, u32[]{:S(2)}, u32[]{:S(2)}) async-start(f32[8,1,3200]{2,1,0:T(1,128)} %broadcast_in_dim.8), calls=%async_computation.3 | async-start | bytes 204800 | tf_op jit(solution)/shard_map/all_to_all | solution.py:104
  216.2 6.0 %all-to-all-done.3 = f32[8,1,3200]{2,1,0:T(1,128)S(1)} async-done(((f32[8,1,3200]{2,1,0:T(1,128)}), f32[8,1,3200]{2,1,0:T(1,128)S(1)}, u32[]{:S(2)}, u32[]{:S(2)}) %all-to-all-start.3) | async-done | bytes 102432 | tf_op jit(solution)/shard_map/all_to_all | solution.py:104
  (88 shorter events, 41.9 us)
Async XLA Ops:
  1.6 35.0 %copy-start.1 = (bf16[3,6,64,256]{3,2,1,0:T(8,128)(2,1)S(1)}, bf16[3,6,64,256]{3,2,1,0:T(8,128)(2,1)}, u32[]{:S(2)}) copy-start(bf16[3,6,64,256]{3,2,1,0:T(8,128)(2,1)} %param.6) | copy-start | bytes 1769476
  2.5 25.3 %all-to-all-start = ((bf16[64,3,640]{2,1,0:T(4,128)(2,1)}), bf16[64,3,640]{2,1,0:T(4,128)(2,1)S(1)}, u32[]{:S(2)}, u32[]{:S(2)}) async-start(bf16[64,3,640]{2,1,0:T(4,128)(2,1)} %pad.4.clone), calls=%async_computation | async-start | bytes 655360 | tf_op jit(solution)/shard_map/all_to_all | solution.py:29
  29.4 25.6 %all-to-all-start.1 = ((bf16[64,6,640]{2,1,0:T(8,128)(2,1)}), bf16[64,6,640]{2,1,0:T(8,128)(2,1)}, u32[]{:S(2)}, u32[]{:S(2)}) async-start(bf16[64,6,640]{2,1,0:T(8,128)(2,1)} %reshape.395), calls=%async_computation.1 | async-start | bytes 1310720 | tf_op jit(solution)/shard_map/all_to_all | solution.py:32
  36.7 1.6 copy-start.2
  36.8 1.6 copy-start.3
  36.9 1.5 copy-start
  56.0 15.3 %collective-permute-start = (bf16[6,8,3200]{2,1,0:T(8,128)(2,1)S(1)}, bf16[6,8,3200]{2,1,0:T(8,128)(2,1)S(1)}, u32[]{:S(2)}, u32[]{:S(2)}) collective-permute-start(bf16[6,8,3200]{2,1,0:T(8,128)(2,1)S(1)} %bitcast.84), channel_id=1, source_target_pairs={{0,1},{1,2},{2,3},{3,0},{4,5},{5,6},{6,7},{7,4},{8,9},{9,10},{10,1... | collective-permute-start | bytes 921608 | tf_op jit(solution)/shard_map/ppermute | solution.py:40
  59.5 14.2 %collective-permute-start.1 = (bf16[6,8,3200]{2,1,0:T(8,128)(2,1)S(1)}, bf16[6,8,3200]{2,1,0:T(8,128)(2,1)S(1)}, u32[]{:S(2)}, u32[]{:S(2)}) collective-permute-start(bf16[6,8,3200]{2,1,0:T(8,128)(2,1)S(1)} %bitcast.85), channel_id=1, source_target_pairs={{0,3},{1,0},{2,1},{3,2},{4,7},{5,4},{6,5},{7,6},{8,11},{9,8},{10,9... | collective-permute-start | bytes 921608 | tf_op jit(solution)/shard_map/ppermute | solution.py:41
  63.1 17.1 %collective-permute-start.4 = (bf16[6,8,3200]{2,1,0:T(8,128)(2,1)S(1)}, bf16[6,8,3200]{2,1,0:T(8,128)(2,1)S(1)}, u32[]{:S(2)}, u32[]{:S(2)}) collective-permute-start(bf16[6,8,3200]{2,1,0:T(8,128)(2,1)S(1)} %bitcast.86), channel_id=1, source_target_pairs={{0,4},{1,5},{2,6},{3,7},{4,0},{5,1},{6,2},{7,3},{8,12},{9,13},{10,... | collective-permute-start | bytes 921608 | tf_op jit(solution)/shard_map/ppermute | solution.py:48
  71.4 16.0 %collective-permute-start.2 = (bf16[3,8,3200]{2,1,0:T(8,128)(2,1)S(1)}, bf16[3,8,3200]{2,1,0:T(8,128)(2,1)S(1)}, u32[]{:S(2)}, u32[]{:S(2)}) collective-permute-start(bf16[3,8,3200]{2,1,0:T(8,128)(2,1)S(1)} %slice.51), channel_id=1, source_target_pairs={{0,1},{1,2},{2,3},{3,0},{4,5},{5,6},{6,7},{7,4},{8,9},{9,10},{10,1... | collective-permute-start | bytes 460808 | tf_op jit(solution)/shard_map/ppermute | solution.py:42
  73.6 28.2 %copy-start.4 = (bf16[8,6,8,256]{3,2,1,0:T(8,128)(2,1)S(1)}, bf16[8,6,8,256]{3,2,1,0:T(8,128)(2,1)}, u32[]{:S(2)}) copy-start(bf16[8,6,8,256]{3,2,1,0:T(8,128)(2,1)} %gather_fusion.1) | copy-start | bytes 589828
  73.6 28.2 %copy-start.8 = (f32[3200]{0:T(1024)S(1)}, f32[3200]{0:T(1024)}, u32[]{:S(2)}) copy-start(f32[3200]{0:T(1024)} %param.9) | copy-start | bytes 38404
  73.7 13.7 %collective-permute-start.3 = (bf16[3,8,3200]{2,1,0:T(8,128)(2,1)S(1)}, bf16[3,8,3200]{2,1,0:T(8,128)(2,1)S(1)}, u32[]{:S(2)}, u32[]{:S(2)}) collective-permute-start(bf16[3,8,3200]{2,1,0:T(8,128)(2,1)S(1)} %slice.52), channel_id=1, source_target_pairs={{0,3},{1,0},{2,1},{3,2},{4,7},{5,4},{6,5},{7,6},{8,11},{9,8},{10,9... | collective-permute-start | bytes 460808 | tf_op jit(solution)/shard_map/ppermute | solution.py:43
  80.3 11.7 %collective-permute-start.5 = (bf16[6,8,3200]{2,1,0:T(8,128)(2,1)S(1)}, bf16[6,8,3200]{2,1,0:T(8,128)(2,1)S(1)}, u32[]{:S(2)}, u32[]{:S(2)}) collective-permute-start(bf16[6,8,3200]{2,1,0:T(8,128)(2,1)S(1)} %collective-permute-done.4), channel_id=1, source_target_pairs={{0,1},{1,2},{2,3},{3,0},{4,5},{5,6},{6,7},{7,4},{8,9},{9,10},{10,1... | collective-permute-start | bytes 921608 | tf_op jit(solution)/shard_map/ppermute | solution.py:40
  82.5 11.4 %collective-permute-start.6 = (bf16[6,8,3200]{2,1,0:T(8,128)(2,1)S(1)}, bf16[6,8,3200]{2,1,0:T(8,128)(2,1)S(1)}, u32[]{:S(2)}, u32[]{:S(2)}) collective-permute-start(bf16[6,8,3200]{2,1,0:T(8,128)(2,1)S(1)} %collective-permute-done.4), channel_id=1, source_target_pairs={{0,3},{1,0},{2,1},{3,2},{4,7},{5,4},{6,5},{7,6},{8,11},{9,8},{10,9... | collective-permute-start | bytes 921608 | tf_op jit(solution)/shard_map/ppermute | solution.py:41
  91.9 8.3 %collective-permute-start.7 = (bf16[3,8,3200]{2,1,0:T(8,128)(2,1)S(1)}, bf16[3,8,3200]{2,1,0:T(8,128)(2,1)S(1)}, u32[]{:S(2)}, u32[]{:S(2)}) collective-permute-start(bf16[3,8,3200]{2,1,0:T(8,128)(2,1)S(1)} %slice.53), channel_id=1, source_target_pairs={{0,1},{1,2},{2,3},{3,0},{4,5},{5,6},{6,7},{7,4},{8,9},{9,10},{10,1... | collective-permute-start | bytes 460808 | tf_op jit(solution)/shard_map/ppermute | solution.py:42
  93.9 7.9 %collective-permute-start.8 = (bf16[3,8,3200]{2,1,0:T(8,128)(2,1)S(1)}, bf16[3,8,3200]{2,1,0:T(8,128)(2,1)S(1)}, u32[]{:S(2)}, u32[]{:S(2)}) collective-permute-start(bf16[3,8,3200]{2,1,0:T(8,128)(2,1)S(1)} %slice.54), channel_id=1, source_target_pairs={{0,3},{1,0},{2,1},{3,2},{4,7},{5,4},{6,5},{7,6},{8,11},{9,8},{10,9... | collective-permute-start | bytes 460808 | tf_op jit(solution)/shard_map/ppermute | solution.py:43
  101.8 2.3 %copy-start.7 = (bf16[8,6,8,3200]{3,2,1,0:T(8,128)(2,1)}, bf16[8,6,8,3200]{3,2,1,0:T(8,128)(2,1)S(1)}, u32[]{:S(2)}) copy-start(bf16[8,6,8,3200]{3,2,1,0:T(8,128)(2,1)S(1)} %fusion.17) | copy-start | bytes 7372804
  110.9 89.7 %all-to-all-start.2 = ((bf16[64,5,3200]{2,1,0:T(8,128)(2,1)}), bf16[64,5,3200]{2,1,0:T(8,128)(2,1)S(1)}, u32[]{:S(2)}, u32[]{:S(2)}) async-start(bf16[64,5,3200]{2,1,0:T(8,128)(2,1)} %pad_maximum_fusion), calls=%async_computation.2 | async-start | bytes 6553600 | tf_op jit(solution)/shard_map/all_to_all | solution.py:100
  201.2 12.3 %copy-start.6 = (bf16[6,64,2,128]{3,1,2,0:T(8,128)(2,1)S(1)}, bf16[6,64,2,128]{3,1,2,0:T(8,128)(2,1)}, u32[]{:S(2)}) copy-start(bf16[6,64,2,128]{3,1,2,0:T(8,128)(2,1)} %fusion.8) | copy-start | bytes 589828
  201.2 13.0 %copy-start.5 = (bf16[6,64,2,128]{3,1,2,0:T(8,128)(2,1)S(1)}, bf16[6,64,2,128]{3,1,2,0:T(8,128)(2,1)}, u32[]{:S(2)}) copy-start(bf16[6,64,2,128]{3,1,2,0:T(8,128)(2,1)} %fusion.11) | copy-start | bytes 589828
  202.0 20.2 %all-to-all-start.3 = ((f32[8,1,3200]{2,1,0:T(1,128)}), f32[8,1,3200]{2,1,0:T(1,128)S(1)}, u32[]{:S(2)}, u32[]{:S(2)}) async-start(f32[8,1,3200]{2,1,0:T(1,128)} %broadcast_in_dim.8), calls=%async_computation.3 | async-start | bytes 204800 | tf_op jit(solution)/shard_map/all_to_all | solution.py:104

commit v2 on v1

--- a/solution.py
+++ b/solution.py
@@ -1,6 +1,8 @@
 import jax
 import jax.numpy as jnp
 from jax import lax
+from jax.experimental import pallas as pl
+from jax.experimental.pallas import tpu as pltpu
 from jax.sharding import PartitionSpec as P
 
 N_X = 4
@@ -35,13 +37,8 @@
 
 
 def ring_gather(block):
-    half = block.shape[0] // 2
-    ahead, behind = tensor_step(0, 1), tensor_step(0, -1)
-    from_left = lax.ppermute(block, "tensor", ahead)
-    from_right = lax.ppermute(block, "tensor", behind)
-    far_low = lax.ppermute(from_left[:half], "tensor", ahead)
-    far_high = lax.ppermute(from_right[half:], "tensor", behind)
-    return [block, from_left, from_right, jnp.concatenate([far_low, far_high])]
+    steps = [lax.ppermute(block, "tensor", tensor_step(0, k)) for k in (1, -1, 2)]
+    return [block] + steps
 
 
 def gather_tokens(block):
@@ -57,14 +54,109 @@
     return jnp.stack(near + far), jnp.stack(places)
 
 
+def replica_step(move):
+    pairs = []
+    for index in range(64):
+        z, y, core = index // 16, index // 2 % 8, index % 2
+        new_z, new_y, new_core = move(z, y, core)
+        pairs.append((index, new_z * 16 + new_y * 2 + new_core))
+    return pairs
+
+
+def over_chip_and_tensor(part):
+    near = [
+        [(chip * 2 + core) * 8 + index for core in range(2) for index in range(8)]
+        for chip in range(32)
+    ]
+    copies = jnp.broadcast_to(part, (16, 1) + part.shape)
+    arrived = lax.all_to_all(copies, ("replica", "tensor"), 0, 0, axis_index_groups=near)
+    return jnp.sum(arrived, axis=(0, 1))
+
+
+def product_body(left_ref, right_ref, weight_ref, gain_ref, given_ref, kept_ref, scale_ref):
+    product = jnp.dot(left_ref[...], right_ref[...], preferred_element_type=jnp.float32)
+    scale_ref[...] = jnp.sum(
+        product * weight_ref[...].astype(jnp.float32), axis=0, keepdims=True
+    )
+    partial = product * gain_ref[...]
+    half = given_ref.shape[0]
+    given_ref[...] = partial[:half].astype(jnp.bfloat16)
+    kept_ref[...] = partial[half:]
+
+
+def weight_products(left, right, weights, gain):
+    rows, depth = left.shape
+    width = right.shape[1]
+    step = width // 5
+    by_column = lambda height: pl.BlockSpec((height, step), lambda i: (0, i))
+    return pl.pallas_call(
+        product_body,
+        grid=(5,),
+        in_specs=[
+            pl.BlockSpec((rows, depth), lambda i: (0, 0)),
+            by_column(depth),
+            by_column(rows),
+            by_column(1),
+        ],
+        out_specs=[by_column(rows // 2), by_column(rows // 2), by_column(1)],
+        out_shape=[
+            jax.ShapeDtypeStruct((rows // 2, width), jnp.bfloat16),
+            jax.ShapeDtypeStruct((rows // 2, width), jnp.float32),
+            jax.ShapeDtypeStruct((1, width), jnp.float32),
+        ],
+        compiler_params=pltpu.CompilerParams(vmem_limit_bytes=24 * 2**20),
+        cost_estimate=pl.CostEstimate(
+            flops=2 * rows * depth * width, bytes_accessed=7 * 2**20, transcendentals=0
+        ),
+        name="weight_products",
+    )(left, right, weights, gain)
+
+
+def outgoing_body(kept_ref, taken_ref, extra_ref, out_ref):
+    width = kept_ref.shape[1]
+    held = out_ref.shape[1]
+    total = kept_ref[...] + taken_ref[...].astype(jnp.float32)
+    for block in range(out_ref.shape[0]):
+        out_ref[block, :, :width] = total[block * held : (block + 1) * held].astype(jnp.bfloat16)
+        out_ref[block, :, width:] = extra_ref[...]
+
+
+def outgoing_blocks(kept, taken, extra):
+    rows, width = kept.shape
+    held, more = extra.shape
+    step = 32
+    by_row = pl.BlockSpec((step, width), lambda i: (i, 0))
+    return pl.pallas_call(
+        outgoing_body,
+        grid=(rows // step,),
+        in_specs=[by_row, by_row, pl.BlockSpec((held, more), lambda i: (0, 0))],
+        out_specs=pl.BlockSpec((step // held, held, width + more), lambda i: (i, 0, 0)),
+        out_shape=jax.ShapeDtypeStruct((rows // held, held, width + more), jnp.bfloat16),
+        compiler_params=pltpu.CompilerParams(vmem_limit_bytes=24 * 2**20),
+        cost_estimate=pl.CostEstimate(
+            flops=rows * width, bytes_accessed=4 * 2**20, transcendentals=0
+        ),
+        name="outgoing_blocks",
+    )(kept, taken, extra)
+
+
 def local(owner, qkv, grad_out, w_out, layer_scale):
     slots, tokens = qkv.shape[1], qkv.shape[2]
     size, heads, width = w_out.shape
     groups = 8
     run = tokens // groups
     factor = size ** (-0.5)
+    rows = size * heads
+    core = lax.axis_index("replica") % 2
 
     dealt = deal(owner, grad_out, slots)
+
+    position = jnp.arange(rows, dtype=jnp.int32)
+    e_of = position % 128 // 4 * 4 + 2 * jnp.where(position < 128, 1 - core, core) + position % 4 // 2
+    h_of = position % 2
+    column = jnp.arange(rows, dtype=jnp.int32)
+    by_head = (column[:, None] == (h_of * size + e_of)[None, :]).astype(jnp.bfloat16)
+    by_size = (column[:, None] == (e_of * heads + h_of)[None, :]).astype(jnp.bfloat16)
 
     block = qkv.reshape(3, slots, tokens, heads, size)
     queries, keys_in, values = block[0], block[1], block[2]
@@ -75,40 +167,53 @@
     probs = raised / jnp.sum(raised, axis=-1, keepdims=True)
     probs_low = probs.astype(jnp.bfloat16)
     attended = jnp.einsum(
-        "mhqk,mkhe->mqeh", probs_low, values, preferred_element_type=jnp.float32
-    ).astype(jnp.bfloat16)
-    weights = w_out.reshape(size * heads, width)
-    scaled_weights = (weights.astype(jnp.float32) * layer_scale).astype(jnp.bfloat16)
+        "mhqk,mkhe->mqhe", probs_low, values, preferred_element_type=jnp.float32
+    ).astype(jnp.bfloat16)
+    weights = jnp.einsum(
+        "wp,wc->pc",
+        by_size,
+        w_out.reshape(rows, width),
+        preferred_element_type=jnp.float32,
+    )
+    scaled_weights = (weights * layer_scale).astype(jnp.bfloat16)
+    sent_order = jnp.einsum(
+        "nw,wp->np",
+        attended.reshape(slots * tokens, rows),
+        by_head,
+        preferred_element_type=jnp.float32,
+    ).astype(jnp.bfloat16)
+    grouped = sent_order.reshape(slots, groups, run, rows).transpose(1, 0, 2, 3)
 
     pieces, places = gather_tokens(dealt)
-    grouped = attended.reshape(slots, groups, run, size * heads).transpose(1, 0, 2, 3)
-    in_order = grouped[places].reshape(groups * slots * run, size * heads)
+    in_order = grouped[places].reshape(groups * slots * run, rows)
     flat = pieces.reshape(groups * slots * run, width)
-    product = jnp.einsum("nw,nc->wc", in_order, flat, preferred_element_type=jnp.float32)
-    partial = (product * layer_scale).astype(jnp.bfloat16)
-    scale_part = jnp.sum(product * weights.astype(jnp.float32), axis=0).astype(jnp.bfloat16)
-
-    replicas = 64
-    rows = size * heads // replicas
-    outgoing = jnp.concatenate(
-        [
-            partial.reshape(replicas, rows, width),
-            jnp.broadcast_to(scale_part, (replicas, 1, width)),
-        ],
-        axis=1,
-    )
-    arrived = lax.all_to_all(outgoing, "replica", 0, 0)
+    given, kept, scale_part = weight_products(
+        in_order.T, flat, weights.astype(jnp.bfloat16), layer_scale[None, :]
+    )
+    taken = lax.ppermute(given, "replica", replica_step(lambda z, y, c: (z, y, 1 - c)))
+    columns = [
+        [z * 16 + y * 2 + c for z in range(4) for y in range(8)] for c in range(2)
+    ]
+    held = rows // 64
+    extra = over_chip_and_tensor(scale_part[0]).astype(jnp.bfloat16)
+    extra = jnp.pad(extra.reshape(held, width // held), ((0, 0), (0, 96)))
+    outgoing = outgoing_blocks(kept, taken, extra)
+    arrived = lax.all_to_all(outgoing, "replica", 0, 0, axis_index_groups=columns)
     summed = jnp.sum(arrived.astype(jnp.float32), axis=0)
-    grad_w = summed[:rows].reshape(size // replicas, heads, width)
-    scale_copies = jnp.broadcast_to(summed[rows], (groups, width))
-    grad_scale = jnp.sum(lax.all_to_all(scale_copies, "tensor", 0, 0), axis=0)
-
+    grad_w = summed[:, :width].reshape(size // 64, heads, width)
+    grad_scale = summed[:, width : width + width // held].reshape(width)
+
+    flat, _ = lax.optimization_barrier((flat, outgoing))
     d_flat = jnp.einsum(
         "nc,wc->nw", flat, scaled_weights, preferred_element_type=jnp.float32
     ).astype(jnp.bfloat16)
-    d_grouped = d_flat.reshape(groups, slots, run, size, heads)
-    back = jnp.argsort(places)
-    d_attended = d_grouped[back].transpose(1, 0, 2, 4, 3).reshape(slots, tokens, heads, size)
+    d_heads = jnp.einsum("np,wp->nw", d_flat, by_head, preferred_element_type=jnp.float32)
+    d_grouped = d_heads.astype(jnp.bfloat16).reshape(groups, slots, run, rows)
+    back = jnp.sum(
+        jnp.where(places[None, :] == jnp.arange(groups)[:, None], jnp.arange(groups)[None, :], 0),
+        axis=1,
+    )
+    d_attended = d_grouped[back].transpose(1, 0, 2, 3).reshape(slots, tokens, heads, size)
     d_values = jnp.einsum(
         "mhqk,mqhe->mkhe", probs_low, d_attended, preferred_element_type=jnp.float32
     ).astype(jnp.bfloat16)

time: 224 us -> 167 us (0.75)
  the two profiles are of different devices: /device:TPU:24 before, /device:TPU:8 now
where the time goes in v2:
time: 167 us; the launch traced here: 166 us
  starting transfers between devices  59.4 us (36%)
  waiting for transfers between devices  54.6 us (33%)
  local copies, waits for them, and re-layouts  16.3 us (10%)
  blocking collectives  13.8 us (8%)
  matrix products  12.9 us (8%)
  Pallas kernels  4.93 us (3%)
  other arithmetic  2.58 us (2%)
    ppermute x6, starting transfers between devices, ring_gather(): lax.ppermute(block, 'tensor', tensor_step(0, k))  19.9 us
    all_to_all x1, waiting for transfers between devices, local(): lax.all_to_all(outgoing, 'replica', 0, 0, axis_index_groups=columns)  17.4 us
    ppermute x6, waiting for transfers between devices, ring_gather(): lax.ppermute(block, 'tensor', tensor_step(0, k))  15.2 us
    all_to_all x1, blocking collectives, over_chip_and_tensor(): lax.all_to_all(copies, ('replica', 'tensor'), 0, 0, axis_index_groups=near)  13.8 us
    all_to_all x1, starting transfers between devices, deal(): lax.all_to_all(pieces, 'replica', 0, 0)  13.5 us
    all_to_all x1, waiting for transfers between devices, deal(): mine = lax.all_to_all(dealt, 'replica', 0, 0)[:tokens * runs]  12.9 us
    all_to_all x1, starting transfers between devices, local(): lax.all_to_all(outgoing, 'replica', 0, 0, axis_index_groups=columns)  10.4 us
    all_to_all x1, waiting for transfers between devices, deal(): lax.all_to_all(pieces, 'replica', 0, 0)  9.15 us
  transfers between devices with their start and end apart: 11, of which 5 were waited for; matrix products, arithmetic and copies ran while one was open for 14% of the time, Pallas kernels for 0%

profile of v2, /device:TPU:8, one launch (start us, length us, event | category | flops | bytes accessed | tf_op | source)
XLA Modules:
  0.0 165.8 jit_solution(12039474428019240473)
XLA Ops:
  2.4 13.5 %all-to-all-start = ((bf16[64,3,640]{2,1,0:T(4,128)(2,1)}), bf16[64,3,640]{2,1,0:T(4,128)(2,1)S(1)}, u32[]{:S(2)}, u32[]{:S(2)}) async-start(bf16[64,3,640]{2,1,0:T(4,128)(2,1)} %pad.8.clone), calls=%async_computation | async-start | bytes 655360 | tf_op jit(solution)/shard_map/all_to_all | solution.py:31
  20.5 9.2 %all-to-all-done = bf16[64,3,640]{2,1,0:T(4,128)(2,1)S(1)} async-done(((bf16[64,3,640]{2,1,0:T(4,128)(2,1)}), bf16[64,3,640]{2,1,0:T(4,128)(2,1)S(1)}, u32[]{:S(2)}, u32[]{:S(2)}) %all-to-all-start) | async-done | bytes 245792 | tf_op jit(solution)/shard_map/all_to_all | solution.py:31
  31.2 5.5 %all-to-all-start.1 = ((bf16[64,6,640]{2,1,0:T(8,128)(2,1)}), bf16[64,6,640]{2,1,0:T(8,128)(2,1)S(1)}, u32[]{:S(2)}, u32[]{:S(2)}) async-start(bf16[64,6,640]{2,1,0:T(8,128)(2,1)} %reshape.471), calls=%async_computation.1 | async-start | bytes 1310720 | tf_op jit(solution)/shard_map/all_to_all | solution.py:34
  37.7 3.7 %reshape.478 = bf16[256,3200]{1,0:T(8,128)(2,1)S(1)} reshape(bf16[128,2,3200]{2,1,0:T(2,128)(2,1)} %param.8) | data formatting | bytes 3276800 | tf_op jit(solution)/shard_map/reshape | solution.py:175
  41.4 2.9 %fusion.81 = (bf16[256,3200]{1,0:T(8,128)(2,1)}, f32[256,3200]{1,0:T(8,128)}) fusion(bf16[256,3200]{1,0:T(8,128)(2,1)S(1)} %reshape.478, s32[256]{0:T(256)S(1)} %get-tuple-element.18), kind=kOutput, calls=%fused_computation.101 | convolution fusion | flops 420315136 | bytes 6554624 | tf_op jit(solution)/shard_map/wp,wc->pc/dot_general | solution.py:172
  44.3 12.9 %all-to-all-done.1 = bf16[64,6,640]{2,1,0:T(8,128)(2,1)S(1)} async-done(((bf16[64,6,640]{2,1,0:T(8,128)(2,1)}), bf16[64,6,640]{2,1,0:T(8,128)(2,1)S(1)}, u32[]{:S(2)}, u32[]{:S(2)}) %all-to-all-start.1) | async-done | bytes 491552 | tf_op jit(solution)/shard_map/all_to_all | solution.py:34
  57.2 8.2 %collective-permute-start.3 = (bf16[6,8,3200]{2,1,0:T(8,128)(2,1)S(1)}, bf16[6,8,3200]{2,1,0:T(8,128)(2,1)S(1)}, u32[]{:S(2)}, u32[]{:S(2)}) collective-permute-start(bf16[6,8,3200]{2,1,0:T(8,128)(2,1)S(1)} %bitcast.83), channel_id=1, source_target_pairs={{0,4},{1,5},{2,6},{3,7},{4,0},{5,1},{6,2},{7,3},{8,12},{9,13},{10,... | collective-permute-start | bytes 921608 | tf_op jit(solution)/shard_map/ppermute | solution.py:45
  65.4 4.9 %collective-permute-start.2 = (bf16[6,8,3200]{2,1,0:T(8,128)(2,1)S(1)}, bf16[6,8,3200]{2,1,0:T(8,128)(2,1)S(1)}, u32[]{:S(2)}, u32[]{:S(2)}) collective-permute-start(bf16[6,8,3200]{2,1,0:T(8,128)(2,1)S(1)} %bitcast.84), channel_id=1, source_target_pairs={{0,2},{1,3},{2,0},{3,1},{4,6},{5,7},{6,4},{7,5},{8,10},{9,11},{10,... | collective-permute-start | bytes 921608 | tf_op jit(solution)/shard_map/ppermute | solution.py:40
  70.4 3.0 %collective-permute-start.1 = (bf16[6,8,3200]{2,1,0:T(8,128)(2,1)S(1)}, bf16[6,8,3200]{2,1,0:T(8,128)(2,1)S(1)}, u32[]{:S(2)}, u32[]{:S(2)}) collective-permute-start(bf16[6,8,3200]{2,1,0:T(8,128)(2,1)S(1)} %bitcast.85), channel_id=1, source_target_pairs={{0,3},{1,0},{2,1},{3,2},{4,7},{5,4},{6,5},{7,6},{8,11},{9,8},{10,9... | collective-permute-start | bytes 921608 | tf_op jit(solution)/shard_map/ppermute | solution.py:40
  73.4 2.8 %collective-permute-start = (bf16[6,8,3200]{2,1,0:T(8,128)(2,1)S(1)}, bf16[6,8,3200]{2,1,0:T(8,128)(2,1)S(1)}, u32[]{:S(2)}, u32[]{:S(2)}) collective-permute-start(bf16[6,8,3200]{2,1,0:T(8,128)(2,1)S(1)} %bitcast.86), channel_id=1, source_target_pairs={{0,1},{1,2},{2,3},{3,0},{4,5},{5,6},{6,7},{7,4},{8,9},{9,10},{10,1... | collective-permute-start | bytes 921608 | tf_op jit(solution)/shard_map/ppermute | solution.py:40
  76.3 2.7 %collective-permute-start.6 = (bf16[6,8,3200]{2,1,0:T(8,128)(2,1)S(1)}, bf16[6,8,3200]{2,1,0:T(8,128)(2,1)S(1)}, u32[]{:S(2)}, u32[]{:S(2)}) collective-permute-start(bf16[6,8,3200]{2,1,0:T(8,128)(2,1)S(1)} %collective-permute-done.3), channel_id=1, source_target_pairs={{0,2},{1,3},{2,0},{3,1},{4,6},{5,7},{6,4},{7,5},{8,10},{9,11},{10,... | collective-permute-start | bytes 921608 | tf_op jit(solution)/shard_map/ppermute | solution.py:40
  79.0 4.5 %collective-permute-start.5 = (bf16[6,8,3200]{2,1,0:T(8,128)(2,1)S(1)}, bf16[6,8,3200]{2,1,0:T(8,128)(2,1)S(1)}, u32[]{:S(2)}, u32[]{:S(2)}) collective-permute-start(bf16[6,8,3200]{2,1,0:T(8,128)(2,1)S(1)} %collective-permute-done.3), channel_id=1, source_target_pairs={{0,3},{1,0},{2,1},{3,2},{4,7},{5,4},{6,5},{7,6},{8,11},{9,8},{10,9... | collective-permute-start | bytes 921608 | tf_op jit(solution)/shard_map/ppermute | solution.py:40
  83.5 7.3 %collective-permute-done = bf16[6,8,3200]{2,1,0:T(8,128)(2,1)S(1)} collective-permute-done((bf16[6,8,3200]{2,1,0:T(8,128)(2,1)S(1)}, bf16[6,8,3200]{2,1,0:T(8,128)(2,1)S(1)}, u32[]{:S(2)}, u32[]{:S(2)}) %collective-permute-start) | collective-permute-done | bytes 307232 | tf_op jit(solution)/shard_map/ppermute | solution.py:40
  90.9 1.9 %collective-permute-start.4 = (bf16[6,8,3200]{2,1,0:T(8,128)(2,1)S(1)}, bf16[6,8,3200]{2,1,0:T(8,128)(2,1)S(1)}, u32[]{:S(2)}, u32[]{:S(2)}) collective-permute-start(bf16[6,8,3200]{2,1,0:T(8,128)(2,1)S(1)} %collective-permute-done.3), channel_id=1, source_target_pairs={{0,1},{1,2},{2,3},{3,0},{4,5},{5,6},{6,7},{7,4},{8,9},{9,10},{10,1... | collective-permute-start | bytes 921608 | tf_op jit(solution)/shard_map/ppermute | solution.py:40
  92.9 7.9 %collective-permute-done.4 = bf16[6,8,3200]{2,1,0:T(8,128)(2,1)S(1)} collective-permute-done((bf16[6,8,3200]{2,1,0:T(8,128)(2,1)S(1)}, bf16[6,8,3200]{2,1,0:T(8,128)(2,1)S(1)}, u32[]{:S(2)}, u32[]{:S(2)}) %collective-permute-start.4) | collective-permute-done | bytes 307232 | tf_op jit(solution)/shard_map/ppermute | solution.py:40
  100.9 3.3 %weight_products.1 = (bf16[128,3200]{1,0:T(8,128)(2,1)}, f32[128,3200]{1,0:T(8,128)S(1)}, f32[1,3200]{1,0:T(1,128)S(1)}) custom-call(bf16[256,384]{1,0:T(8,128)(2,1)S(1)} %bitcast.81, bf16[384,3200]{1,0:T(8,128)(2,1)S(1)} %bitcast.79, bf16[256,3200]{1,0:T(8,128)(2,1)S(1)} %copy-done, f32[1,3200]{1,0:T(1,128)S(1)} %broadcast_in_dim.22.gain_ref), custom_call_target="tpu_custom_call" | custom-call | flops 629145600 | bytes 7340032 | tf_op jit(solution)/shard_map/weight_products/pallas_call | solution.py:92
  105.4 1.9 %collective-permute-start.7 = (bf16[128,3200]{1,0:T(8,128)(2,1)}, bf16[128,3200]{1,0:T(8,128)(2,1)S(1)}, u32[]{:S(2)}, u32[]{:S(2)}) collective-permute-start(bf16[128,3200]{1,0:T(8,128)(2,1)} %get-tuple-element.8), channel_id=1, source_target_pairs={{0,8},{8,0},{16,24},{24,16},{32,40},{40,32},{48,56},{56,48},{64,72... | collective-permute-start | bytes 2457608 | tf_op jit(solution)/shard_map/ppermute | solution.py:193
  107.5 13.8 %all_to_all.20 = f32[16,1,3200]{2,1,0:T(1,128)S(1)} all-to-all(f32[16,1,3200]{2,1,0:T(1,128)S(1)} %broadcast_in_dim.23), channel_id=1, replica_groups={{0,1,2,3,4,5,6,7,8,9,10,11,12,13,14,15},{16,17,18,19,20,21,22,23,24,25,..., dimensions={0} | all-to-all | bytes 409600 | tf_op jit(solution)/shard_map/all_to_all | solution.py:72
  122.9 1.6 outgoing_blocks.1
  124.6 10.4 %all-to-all-start.3 = ((bf16[32,4,4096]{2,1,0:T(4,128)(2,1)}), bf16[32,4,4096]{2,1,0:T(4,128)(2,1)S(1)}, u32[]{:S(2)}, u32[]{:S(2)}) async-start(bf16[32,4,4096]{2,1,0:T(4,128)(2,1)} %outgoing_blocks.1), calls=%async_computation.3 | async-start | bytes 2097152 | tf_op jit(solution)/shard_map/all_to_all | solution.py:201
  135.0 3.6 %convolution_convert_fusion.4 = bf16[384,256]{1,0:T(8,128)(2,1)} fusion(bf16[384,3200]{1,0:T(8,128)(2,1)S(1)} %bitcast.80, f32[256,3200]{1,0:T(8,128)} %get-tuple-element.17, f32[3200]{0:T(1024)S(1)} %copy-done.8, s32[256]{0:T(256)S(1)} %get-tuple-element.19), kind=kOutput, calls=%fused_computation.20 | convolution fusion | flops 681377792 | bytes 5944832 | tf_op jit(solution)/shard_map/np,wp->nw/dot_general | solution.py:210
  138.6 1.5 gather_fusion.1
  141.4 1.4 fusion.13
  146.6 17.4 %all-to-all-done.3 = bf16[32,4,4096]{2,1,0:T(4,128)(2,1)S(1)} async-done(((bf16[32,4,4096]{2,1,0:T(4,128)(2,1)}), bf16[32,4,4096]{2,1,0:T(4,128)(2,1)S(1)}, u32[]{:S(2)}, u32[]{:S(2)}) %all-to-all-start.3) | async-done | bytes 1048608 | tf_op jit(solution)/shard_map/all_to_all | solution.py:201
  (84 shorter events, 18.6 us)
Async XLA Ops:
  2.4 27.2 %all-to-all-start = ((bf16[64,3,640]{2,1,0:T(4,128)(2,1)}), bf16[64,3,640]{2,1,0:T(4,128)(2,1)S(1)}, u32[]{:S(2)}, u32[]{:S(2)}) async-start(bf16[64,3,640]{2,1,0:T(4,128)(2,1)} %pad.8.clone), calls=%async_computation | async-start | bytes 655360 | tf_op jit(solution)/shard_map/all_to_all | solution.py:31
  18.1 2.1 %copy-start.9 = (s32[192]{0:T(256)S(1)}, s32[192]{0:T(256)}, u32[]{:S(2)}) copy-start(s32[192]{0:T(256)} %param.5) | copy-start | bytes 2308
  18.2 2.3 %copy-start.4 = (bf16[6,64,2,128]{3,2,1,0:T(2,128)(2,1)}, bf16[6,64,2,128]{3,2,1,0:T(2,128)(2,1)S(1)}, u32[]{:S(2)}) copy-start(bf16[6,64,2,128]{3,2,1,0:T(2,128)(2,1)S(1)} %squeeze.12) | copy-start | bytes 589828
  18.2 2.2 %copy-start.6 = (bf16[6,64,2,128]{3,2,1,0:T(2,128)(2,1)}, bf16[6,64,2,128]{3,2,1,0:T(2,128)(2,1)S(1)}, u32[]{:S(2)}) copy-start(bf16[6,64,2,128]{3,2,1,0:T(2,128)(2,1)S(1)} %squeeze.13) | copy-start | bytes 589828
  18.3 2.2 %copy-start.3 = (bf16[6,64,2,128]{3,2,1,0:T(2,128)(2,1)}, bf16[6,64,2,128]{3,2,1,0:T(2,128)(2,1)S(1)}, u32[]{:S(2)}) copy-start(bf16[6,64,2,128]{3,2,1,0:T(2,128)(2,1)S(1)} %squeeze.14) | copy-start | bytes 589828
  19.8 17.0 %copy-start.8 = (f32[3200]{0:T(1024)S(1)}, f32[3200]{0:T(1024)}, u32[]{:S(2)}) copy-start(f32[3200]{0:T(1024)} %param.9) | copy-start | bytes 38404
  31.2 26.0 %all-to-all-start.1 = ((bf16[64,6,640]{2,1,0:T(8,128)(2,1)}), bf16[64,6,640]{2,1,0:T(8,128)(2,1)S(1)}, u32[]{:S(2)}, u32[]{:S(2)}) async-start(bf16[64,6,640]{2,1,0:T(8,128)(2,1)} %reshape.471), calls=%async_computation.1 | async-start | bytes 1310720 | tf_op jit(solution)/shard_map/all_to_all | solution.py:34
  57.2 19.1 %collective-permute-start.3 = (bf16[6,8,3200]{2,1,0:T(8,128)(2,1)S(1)}, bf16[6,8,3200]{2,1,0:T(8,128)(2,1)S(1)}, u32[]{:S(2)}, u32[]{:S(2)}) collective-permute-start(bf16[6,8,3200]{2,1,0:T(8,128)(2,1)S(1)} %bitcast.83), channel_id=1, source_target_pairs={{0,4},{1,5},{2,6},{3,7},{4,0},{5,1},{6,2},{7,3},{8,12},{9,13},{10,... | collective-permute-start | bytes 921608 | tf_op jit(solution)/shard_map/ppermute | solution.py:45
  65.4 27.4 %collective-permute-start.2 = (bf16[6,8,3200]{2,1,0:T(8,128)(2,1)S(1)}, bf16[6,8,3200]{2,1,0:T(8,128)(2,1)S(1)}, u32[]{:S(2)}, u32[]{:S(2)}) collective-permute-start(bf16[6,8,3200]{2,1,0:T(8,128)(2,1)S(1)} %bitcast.84), channel_id=1, source_target_pairs={{0,2},{1,3},{2,0},{3,1},{4,6},{5,7},{6,4},{7,5},{8,10},{9,11},{10,... | collective-permute-start | bytes 921608 | tf_op jit(solution)/shard_map/ppermute | solution.py:40
  70.4 22.4 %collective-permute-start.1 = (bf16[6,8,3200]{2,1,0:T(8,128)(2,1)S(1)}, bf16[6,8,3200]{2,1,0:T(8,128)(2,1)S(1)}, u32[]{:S(2)}, u32[]{:S(2)}) collective-permute-start(bf16[6,8,3200]{2,1,0:T(8,128)(2,1)S(1)} %bitcast.85), channel_id=1, source_target_pairs={{0,3},{1,0},{2,1},{3,2},{4,7},{5,4},{6,5},{7,6},{8,11},{9,8},{10,9... | collective-permute-start | bytes 921608 | tf_op jit(solution)/shard_map/ppermute | solution.py:40
  73.4 17.4 %collective-permute-start = (bf16[6,8,3200]{2,1,0:T(8,128)(2,1)S(1)}, bf16[6,8,3200]{2,1,0:T(8,128)(2,1)S(1)}, u32[]{:S(2)}, u32[]{:S(2)}) collective-permute-start(bf16[6,8,3200]{2,1,0:T(8,128)(2,1)S(1)} %bitcast.86), channel_id=1, source_target_pairs={{0,1},{1,2},{2,3},{3,0},{4,5},{5,6},{6,7},{7,4},{8,9},{9,10},{10,1... | collective-permute-start | bytes 921608 | tf_op jit(solution)/shard_map/ppermute | solution.py:40
  76.2 24.7 %copy-start = (bf16[256,3200]{1,0:T(8,128)(2,1)S(1)}, bf16[256,3200]{1,0:T(8,128)(2,1)}, u32[]{:S(2)}) copy-start(bf16[256,3200]{1,0:T(8,128)(2,1)} %get-tuple-element.16.weight_ref) | copy-start | bytes 4915204
  76.3 24.6 %collective-permute-start.6 = (bf16[6,8,3200]{2,1,0:T(8,128)(2,1)S(1)}, bf16[6,8,3200]{2,1,0:T(8,128)(2,1)S(1)}, u32[]{:S(2)}, u32[]{:S(2)}) collective-permute-start(bf16[6,8,3200]{2,1,0:T(8,128)(2,1)S(1)} %collective-permute-done.3), channel_id=1, source_target_pairs={{0,2},{1,3},{2,0},{3,1},{4,6},{5,7},{6,4},{7,5},{8,10},{9,11},{10,... | collective-permute-start | bytes 921608 | tf_op jit(solution)/shard_map/ppermute | solution.py:40
  79.0 21.9 %collective-permute-start.5 = (bf16[6,8,3200]{2,1,0:T(8,128)(2,1)S(1)}, bf16[6,8,3200]{2,1,0:T(8,128)(2,1)S(1)}, u32[]{:S(2)}, u32[]{:S(2)}) collective-permute-start(bf16[6,8,3200]{2,1,0:T(8,128)(2,1)S(1)} %collective-permute-done.3), channel_id=1, source_target_pairs={{0,3},{1,0},{2,1},{3,2},{4,7},{5,4},{6,5},{7,6},{8,11},{9,8},{10,9... | collective-permute-start | bytes 921608 | tf_op jit(solution)/shard_map/ppermute | solution.py:40
  90.9 9.9 %collective-permute-start.4 = (bf16[6,8,3200]{2,1,0:T(8,128)(2,1)S(1)}, bf16[6,8,3200]{2,1,0:T(8,128)(2,1)S(1)}, u32[]{:S(2)}, u32[]{:S(2)}) collective-permute-start(bf16[6,8,3200]{2,1,0:T(8,128)(2,1)S(1)} %collective-permute-done.3), channel_id=1, source_target_pairs={{0,1},{1,2},{2,3},{3,0},{4,5},{5,6},{6,7},{7,4},{8,9},{9,10},{10,1... | collective-permute-start | bytes 921608 | tf_op jit(solution)/shard_map/ppermute | solution.py:40
  104.2 1.2 copy-start.1
  105.4 16.1 %collective-permute-start.7 = (bf16[128,3200]{1,0:T(8,128)(2,1)}, bf16[128,3200]{1,0:T(8,128)(2,1)S(1)}, u32[]{:S(2)}, u32[]{:S(2)}) collective-permute-start(bf16[128,3200]{1,0:T(8,128)(2,1)} %get-tuple-element.8), channel_id=1, source_target_pairs={{0,8},{8,0},{16,24},{24,16},{32,40},{40,32},{48,56},{56,48},{64,72... | collective-permute-start | bytes 2457608 | tf_op jit(solution)/shard_map/ppermute | solution.py:193
  121.5 1.4 copy-start.2
  124.6 39.4 %all-to-all-start.3 = ((bf16[32,4,4096]{2,1,0:T(4,128)(2,1)}), bf16[32,4,4096]{2,1,0:T(4,128)(2,1)S(1)}, u32[]{:S(2)}, u32[]{:S(2)}) async-start(bf16[32,4,4096]{2,1,0:T(4,128)(2,1)} %outgoing_blocks.1), calls=%async_computation.3 | async-start | bytes 2097152 | tf_op jit(solution)/shard_map/all_to_all | solution.py:201
  138.6 4.6 %copy-start.7 = (bf16[6,64,2,128]{3,2,1,0:T(2,128)(2,1)S(1)}, bf16[6,64,2,128]{3,2,1,0:T(2,128)(2,1)}, u32[]{:S(2)}) copy-start(bf16[6,64,2,128]{3,2,1,0:T(2,128)(2,1)} %copy-done.6) | copy-start | bytes 589828
  142.8 2.2 %copy-start.5 = (bf16[6,64,2,128]{3,2,1,0:T(2,128)(2,1)S(1)}, bf16[6,64,2,128]{3,2,1,0:T(2,128)(2,1)}, u32[]{:S(2)}) copy-start(bf16[6,64,2,128]{3,2,1,0:T(2,128)(2,1)} %copy-done.4) | copy-start | bytes 589828

commit v3 on v2

--- a/solution.py
+++ b/solution.py
@@ -17,22 +17,26 @@
 
 
 def deal(owner, grad_out, slot_count):
-    replicas, runs = 64, 5
+    replicas, part, lanes = 64, 4, 128
     images, tokens, width = grad_out.shape
+    parts, runs = tokens // part, width // lanes
+    pieces = parts * runs
     ids = jnp.arange(replicas * images, dtype=jnp.int32)
     same = (owner[:, None] == owner[None, :]) & (ids[None, :] < ids[:, None])
     slot_of = owner * slot_count + jnp.sum(same.astype(jnp.int32), axis=1)
-    slots = jnp.arange(replicas * slot_count, dtype=jnp.int32)
-    chosen = (slots[:, None] == slot_of[None, :]).astype(grad_out.dtype)
-
-    pieces = grad_out.reshape(images, tokens, runs, width // runs).transpose(1, 2, 0, 3)
-    pieces = pieces.reshape(tokens * runs, images, width // runs)
-    pieces = jnp.pad(pieces, ((0, replicas - tokens * runs), (0, 0), (0, 0)))
-    held = lax.all_to_all(pieces, "replica", 0, 0).reshape(replicas * images, width // runs)
+    padded = jnp.pad(slot_of.reshape(replicas, images), ((0, 0), (0, 1)), constant_values=-1)
+    row_of = (padded[:, :, None] * part + jnp.arange(part, dtype=jnp.int32)).reshape(-1)
+    rows = jnp.arange(replicas * slot_count * part, dtype=jnp.int32)
+    chosen = (rows[:, None] == row_of[None, :]).astype(grad_out.dtype)
+
+    spread = grad_out.reshape(images, parts, part, runs, lanes).transpose(3, 1, 0, 2, 4)
+    spread = spread.reshape(pieces, images * part, lanes)
+    spread = jnp.pad(spread, ((0, replicas - pieces), (0, part), (0, 0)))
+    held = lax.all_to_all(spread, "replica", 0, 0).reshape(replicas * (images + 1) * part, lanes)
     dealt = jnp.einsum("mi,ic->mc", chosen, held, preferred_element_type=jnp.float32)
-    dealt = dealt.astype(grad_out.dtype).reshape(replicas, slot_count, width // runs)
-    mine = lax.all_to_all(dealt, "replica", 0, 0)[: tokens * runs]
-    mine = mine.reshape(tokens, runs, slot_count, width // runs).transpose(2, 0, 1, 3)
+    dealt = dealt.astype(grad_out.dtype).reshape(replicas, slot_count * part, lanes)
+    mine = lax.all_to_all(dealt, "replica", 0, 0)[:pieces]
+    mine = mine.reshape(runs, parts, slot_count, part, lanes).transpose(2, 1, 3, 0, 4)
     return mine.reshape(slot_count, tokens, width)
 
 
@@ -81,7 +85,7 @@
     partial = product * gain_ref[...]
     half = given_ref.shape[0]
     given_ref[...] = partial[:half].astype(jnp.bfloat16)
-    kept_ref[...] = partial[half:]
+    kept_ref[...] = partial[half:].astype(jnp.bfloat16)
 
 
 def weight_products(left, right, weights, gain):
@@ -101,7 +105,7 @@
         out_specs=[by_column(rows // 2), by_column(rows // 2), by_column(1)],
         out_shape=[
             jax.ShapeDtypeStruct((rows // 2, width), jnp.bfloat16),
-            jax.ShapeDtypeStruct((rows // 2, width), jnp.float32),
+            jax.ShapeDtypeStruct((rows // 2, width), jnp.bfloat16),
             jax.ShapeDtypeStruct((1, width), jnp.float32),
         ],
         compiler_params=pltpu.CompilerParams(vmem_limit_bytes=24 * 2**20),
@@ -115,7 +119,7 @@
 def outgoing_body(kept_ref, taken_ref, extra_ref, out_ref):
     width = kept_ref.shape[1]
     held = out_ref.shape[1]
-    total = kept_ref[...] + taken_ref[...].astype(jnp.float32)
+    total = kept_ref[...].astype(jnp.float32) + taken_ref[...].astype(jnp.float32)
     for block in range(out_ref.shape[0]):
         out_ref[block, :, :width] = total[block * held : (block + 1) * held].astype(jnp.bfloat16)
         out_ref[block, :, width:] = extra_ref[...]

time: 167 us -> 162 us (0.970)
  waiting for transfers between devices: 54.6 us -> 48.5 us
  local copies, waits for them, and re-layouts: 16.3 us -> 12.1 us
  Pallas kernels: 4.93 us -> 6.75 us
  other arithmetic: 2.58 us -> 4.32 us
  matrix products: 12.9 us -> 14.6 us
    all_to_all x2, waiting for transfers between devices: 22 us -> 15.3 us  [the longest x1 7.77 us: deal(): lax.all_to_all(spread, 'replica', 0, 0)]
    unnamed x28 -> x25, local copies, waits for them, and re-layouts: 3.82 us -> 0.35 us
    pallas_call x1, Pallas kernels: 1.62 us -> 3.41 us  [outgoing_blocks(): pl.pallas_call(outgoing_body, grid=(rows // step,), in_specs=[by_row, by_...]
  transfers between devices with their start and end apart: 11 -> 11, of which waited for: 5 -> 5; matrix products, arithmetic and copies ran while one was open for 14% -> 15% of each run, Pallas kernels for 0% -> 0%
where the time goes in v3:
time: 162 us; the launch traced here: 161 us
  starting transfers between devices  58.9 us (36%)
  waiting for transfers between devices  48.5 us (30%)
  matrix products  14.6 us (9%)
  blocking collectives  14.4 us (9%)
  local copies, waits for them, and re-layouts  12.1 us (7%)
  Pallas kernels  6.75 us (4%)
  other arithmetic  4.32 us (3%)
    ppermute x6, starting transfers between devices, ring_gather(): lax.ppermute(block, 'tensor', tensor_step(0, k))  19.8 us
    all_to_all x1, waiting for transfers between devices, local(): lax.all_to_all(outgoing, 'replica', 0, 0, axis_index_groups=columns)  17.3 us
    ppermute x6, waiting for transfers between devices, ring_gather(): lax.ppermute(block, 'tensor', tensor_step(0, k))  15.8 us
    all_to_all x1, blocking collectives, over_chip_and_tensor(): lax.all_to_all(copies, ('replica', 'tensor'), 0, 0, axis_index_groups=near)  14.4 us
    all_to_all x1, starting transfers between devices, deal(): lax.all_to_all(spread, 'replica', 0, 0)  13.5 us
    all_to_all x1, starting transfers between devices, local(): lax.all_to_all(outgoing, 'replica', 0, 0, axis_index_groups=columns)  9.98 us
    ppermute x1, starting transfers between devices, gather_tokens(): other = lax.ppermute(block, 'tensor', tensor_step(1, 0))  8.35 us
    all_to_all x1, waiting for transfers between devices, deal(): lax.all_to_all(spread, 'replica', 0, 0)  7.77 us
  transfers between devices with their start and end apart: 11, of which 5 were waited for; matrix products, arithmetic and copies ran while one was open for 15% of the time, Pallas kernels for 0%

profile of v3, /device:TPU:8, one launch (start us, length us, event | category | flops | bytes accessed | tf_op | source)
XLA Modules:
  0.0 160.8 jit_solution(15823179669747741379)
XLA Ops:
  2.6 13.5 %all-to-all-start = ((bf16[64,16,128]{2,1,0:T(8,128)(2,1)}), bf16[64,16,128]{2,1,0:T(8,128)(2,1)S(1)}, u32[]{:S(2)}, u32[]{:S(2)}) async-start(bf16[64,16,128]{2,1,0:T(8,128)(2,1)} %pad.13.clone), calls=%async_computation | async-start | bytes 524288 | tf_op jit(solution)/shard_map/all_to_all | solution.py:35
  20.7 7.8 %all-to-all-done = bf16[64,16,128]{2,1,0:T(8,128)(2,1)S(1)} async-done(((bf16[64,16,128]{2,1,0:T(8,128)(2,1)}), bf16[64,16,128]{2,1,0:T(8,128)(2,1)S(1)}, u32[]{:S(2)}, u32[]{:S(2)}) %all-to-all-start) | async-done | bytes 262176 | tf_op jit(solution)/shard_map/all_to_all | solution.py:35
  28.5 1.9 %fusion.4 = bf16[1536,128]{1,0:T(8,128)(2,1)} fusion(bf16[1024,128]{1,0:T(8,128)(2,1)S(1)} %bitcast.84, s32[1024]{0:T(1024)S(1)} %add.216), kind=kOutput, calls=%fused_computation.8 | convolution fusion | flops 404422656 | bytes 659456 | tf_op jit(solution)/shard_map/mi,ic->mc/dot_general | solution.py:36
  30.4 5.4 %all-to-all-start.1 = ((bf16[64,24,128]{2,1,0:T(8,128)(2,1)}), bf16[64,24,128]{2,1,0:T(8,128)(2,1)S(1)}, u32[]{:S(2)}, u32[]{:S(2)}) async-start(bf16[64,24,128]{2,1,0:T(8,128)(2,1)} %bitcast.2), calls=%async_computation.1 | async-start | bytes 786432 | tf_op jit(solution)/shard_map/all_to_all | solution.py:38
  36.7 3.7 %reshape.497 = bf16[256,3200]{1,0:T(8,128)(2,1)S(1)} reshape(bf16[128,2,3200]{2,1,0:T(2,128)(2,1)} %param.8) | data formatting | bytes 3276800 | tf_op jit(solution)/shard_map/reshape | solution.py:179
  40.4 2.9 %fusion.83 = (bf16[256,3200]{1,0:T(8,128)(2,1)}, f32[256,3200]{1,0:T(8,128)}) fusion(bf16[256,3200]{1,0:T(8,128)(2,1)S(1)} %reshape.497, s32[256]{0:T(256)S(1)} %get-tuple-element.18), kind=kOutput, calls=%fused_computation.104 | convolution fusion | flops 420315136 | bytes 6554624 | tf_op jit(solution)/shard_map/wp,wc->pc/dot_general | solution.py:176
  43.3 7.5 %all-to-all-done.1 = bf16[64,24,128]{2,1,0:T(8,128)(2,1)S(1)} async-done(((bf16[64,24,128]{2,1,0:T(8,128)(2,1)}), bf16[64,24,128]{2,1,0:T(8,128)(2,1)S(1)}, u32[]{:S(2)}, u32[]{:S(2)}) %all-to-all-start.1) | async-done | bytes 393248 | tf_op jit(solution)/shard_map/all_to_all | solution.py:38
  51.3 8.4 %collective-permute-start.3 = (bf16[6,8,3200]{2,1,0:T(8,128)(2,1)S(1)}, bf16[6,8,3200]{2,1,0:T(8,128)(2,1)S(1)}, u32[]{:S(2)}, u32[]{:S(2)}) collective-permute-start(bf16[6,8,3200]{2,1,0:T(8,128)(2,1)S(1)} %reshape.492), channel_id=1, source_target_pairs={{0,4},{1,5},{2,6},{3,7},{4,0},{5,1},{6,2},{7,3},{8,12},{9,13},{10,... | collective-permute-start | bytes 921608 | tf_op jit(solution)/shard_map/ppermute | solution.py:49
  59.6 4.9 %collective-permute-start.2 = (bf16[6,8,3200]{2,1,0:T(8,128)(2,1)S(1)}, bf16[6,8,3200]{2,1,0:T(8,128)(2,1)S(1)}, u32[]{:S(2)}, u32[]{:S(2)}) collective-permute-start(bf16[6,8,3200]{2,1,0:T(8,128)(2,1)S(1)} %reshape.492), channel_id=1, source_target_pairs={{0,2},{1,3},{2,0},{3,1},{4,6},{5,7},{6,4},{7,5},{8,10},{9,11},{10,... | collective-permute-start | bytes 921608 | tf_op jit(solution)/shard_map/ppermute | solution.py:44
  64.6 3.0 %collective-permute-start.1 = (bf16[6,8,3200]{2,1,0:T(8,128)(2,1)S(1)}, bf16[6,8,3200]{2,1,0:T(8,128)(2,1)S(1)}, u32[]{:S(2)}, u32[]{:S(2)}) collective-permute-start(bf16[6,8,3200]{2,1,0:T(8,128)(2,1)S(1)} %reshape.492), channel_id=1, source_target_pairs={{0,3},{1,0},{2,1},{3,2},{4,7},{5,4},{6,5},{7,6},{8,11},{9,8},{10,9... | collective-permute-start | bytes 921608 | tf_op jit(solution)/shard_map/ppermute | solution.py:44
  67.6 2.8 %collective-permute-start = (bf16[6,8,3200]{2,1,0:T(8,128)(2,1)S(1)}, bf16[6,8,3200]{2,1,0:T(8,128)(2,1)S(1)}, u32[]{:S(2)}, u32[]{:S(2)}) collective-permute-start(bf16[6,8,3200]{2,1,0:T(8,128)(2,1)S(1)} %reshape.492), channel_id=1, source_target_pairs={{0,1},{1,2},{2,3},{3,0},{4,5},{5,6},{6,7},{7,4},{8,9},{9,10},{10,1... | collective-permute-start | bytes 921608 | tf_op jit(solution)/shard_map/ppermute | solution.py:44
  70.5 2.6 %collective-permute-start.6 = (bf16[6,8,3200]{2,1,0:T(8,128)(2,1)S(1)}, bf16[6,8,3200]{2,1,0:T(8,128)(2,1)S(1)}, u32[]{:S(2)}, u32[]{:S(2)}) collective-permute-start(bf16[6,8,3200]{2,1,0:T(8,128)(2,1)S(1)} %collective-permute-done.3), channel_id=1, source_target_pairs={{0,2},{1,3},{2,0},{3,1},{4,6},{5,7},{6,4},{7,5},{8,10},{9,11},{10,... | collective-permute-start | bytes 921608 | tf_op jit(solution)/shard_map/ppermute | solution.py:44
  73.0 4.5 %collective-permute-start.5 = (bf16[6,8,3200]{2,1,0:T(8,128)(2,1)S(1)}, bf16[6,8,3200]{2,1,0:T(8,128)(2,1)S(1)}, u32[]{:S(2)}, u32[]{:S(2)}) collective-permute-start(bf16[6,8,3200]{2,1,0:T(8,128)(2,1)S(1)} %collective-permute-done.3), channel_id=1, source_target_pairs={{0,3},{1,0},{2,1},{3,2},{4,7},{5,4},{6,5},{7,6},{8,11},{9,8},{10,9... | collective-permute-start | bytes 921608 | tf_op jit(solution)/shard_map/ppermute | solution.py:44
  77.6 8.0 %collective-permute-done = bf16[6,8,3200]{2,1,0:T(8,128)(2,1)S(1)} collective-permute-done((bf16[6,8,3200]{2,1,0:T(8,128)(2,1)S(1)}, bf16[6,8,3200]{2,1,0:T(8,128)(2,1)S(1)}, u32[]{:S(2)}, u32[]{:S(2)}) %collective-permute-start) | collective-permute-done | bytes 307232 | tf_op jit(solution)/shard_map/ppermute | solution.py:44
  85.5 1.9 %collective-permute-start.4 = (bf16[6,8,3200]{2,1,0:T(8,128)(2,1)S(1)}, bf16[6,8,3200]{2,1,0:T(8,128)(2,1)S(1)}, u32[]{:S(2)}, u32[]{:S(2)}) collective-permute-start(bf16[6,8,3200]{2,1,0:T(8,128)(2,1)S(1)} %collective-permute-done.3), channel_id=1, source_target_pairs={{0,1},{1,2},{2,3},{3,0},{4,5},{5,6},{6,7},{7,4},{8,9},{9,10},{10,1... | collective-permute-start | bytes 921608 | tf_op jit(solution)/shard_map/ppermute | solution.py:44
  87.6 7.9 %collective-permute-done.4 = bf16[6,8,3200]{2,1,0:T(8,128)(2,1)S(1)} collective-permute-done((bf16[6,8,3200]{2,1,0:T(8,128)(2,1)S(1)}, bf16[6,8,3200]{2,1,0:T(8,128)(2,1)S(1)}, u32[]{:S(2)}, u32[]{:S(2)}) %collective-permute-start.4) | collective-permute-done | bytes 307232 | tf_op jit(solution)/shard_map/ppermute | solution.py:44
  95.6 3.3 %weight_products.1 = (bf16[128,3200]{1,0:T(8,128)(2,1)}, bf16[128,3200]{1,0:T(8,128)(2,1)S(1)}, f32[1,3200]{1,0:T(1,128)S(1)}) custom-call(bf16[256,384]{1,0:T(8,128)(2,1)S(1)} %bitcast.77, bf16[384,3200]{1,0:T(8,128)(2,1)S(1)} %bitcast.75, bf16[256,3200]{1,0:T(8,128)(2,1)S(1)} %copy-done, f32[1,3200]{1,0:T(1,128)S(1)} %broadcast_in_dim.22.gain_ref), custom_call_target="tpu_custom_call" | custom-call | flops 629145600 | bytes 7340032 | tf_op jit(solution)/shard_map/weight_products/pallas_call | solution.py:96
  98.9 1.9 %collective-permute-start.7 = (bf16[128,3200]{1,0:T(8,128)(2,1)}, bf16[128,3200]{1,0:T(8,128)(2,1)}, u32[]{:S(2)}, u32[]{:S(2)}) collective-permute-start(bf16[128,3200]{1,0:T(8,128)(2,1)} %get-tuple-element.8), channel_id=1, source_target_pairs={{0,8},{8,0},{16,24},{24,16},{32,40},{40,32},{48,56},{56,48},{64,72... | collective-permute-start | bytes 2457608 | tf_op jit(solution)/shard_map/ppermute | solution.py:197
  101.0 14.4 %all_to_all.20 = f32[16,1,3200]{2,1,0:T(1,128)} all-to-all(f32[16,1,3200]{2,1,0:T(1,128)S(1)} %broadcast_in_dim.23), channel_id=1, replica_groups={{0,1,2,3,4,5,6,7,8,9,10,11,12,13,14,15},{16,17,18,19,20,21,22,23,24,25,..., dimensions={0} | all-to-all | bytes 409600 | tf_op jit(solution)/shard_map/all_to_all | solution.py:76
  116.6 3.4 %outgoing_blocks.1 = bf16[32,4,4096]{2,1,0:T(4,128)(2,1)} custom-call(bf16[128,3200]{1,0:T(8,128)(2,1)S(1)} %get-tuple-element.7.kept_ref, bf16[128,3200]{1,0:T(8,128)(2,1)} %collective-permute-done.7.taken_ref, bf16[4,896]{1,0:T(4,128)(2,1)S(1)} %pad.14.extra_ref), custom_call_target="tpu_custom_call" | custom-call | flops 409600 | bytes 4194304 | tf_op jit(solution)/shard_map/outgoing_blocks/pallas_call | solution.py:133
  120.0 10.0 %all-to-all-start.3 = ((bf16[32,4,4096]{2,1,0:T(4,128)(2,1)}), bf16[32,4,4096]{2,1,0:T(4,128)(2,1)S(1)}, u32[]{:S(2)}, u32[]{:S(2)}) async-start(bf16[32,4,4096]{2,1,0:T(4,128)(2,1)} %outgoing_blocks.1), calls=%async_computation.3 | async-start | bytes 2097152 | tf_op jit(solution)/shard_map/all_to_all | solution.py:205
  130.0 3.6 %convolution_convert_fusion.3 = bf16[384,256]{1,0:T(8,128)(2,1)} fusion(bf16[384,3200]{1,0:T(8,128)(2,1)S(1)} %bitcast.76, f32[256,3200]{1,0:T(8,128)} %get-tuple-element.17, f32[3200]{0:T(1024)S(1)} %copy-done.7, s32[256]{0:T(256)S(1)} %get-tuple-element.19), kind=kOutput, calls=%fused_computation.23 | convolution fusion | flops 681377792 | bytes 5944832 | tf_op jit(solution)/shard_map/np,wp->nw/dot_general | solution.py:214
  133.7 1.5 gather_fusion.1
  141.7 17.3 %all-to-all-done.3 = bf16[32,4,4096]{2,1,0:T(4,128)(2,1)S(1)} async-done(((bf16[32,4,4096]{2,1,0:T(4,128)(2,1)}), bf16[32,4,4096]{2,1,0:T(4,128)(2,1)S(1)}, u32[]{:S(2)}, u32[]{:S(2)}) %all-to-all-start.3) | async-done | bytes 1048608 | tf_op jit(solution)/shard_map/all_to_all | solution.py:205
  (86 shorter events, 17.4 us)
Async XLA Ops:
  0.6 17.6 %copy-start.2 = (bf16[3,6,64,256]{3,2,1,0:T(8,128)(2,1)S(1)}, bf16[3,6,64,256]{3,2,1,0:T(8,128)(2,1)}, u32[]{:S(2)}) copy-start(bf16[3,6,64,256]{3,2,1,0:T(8,128)(2,1)} %param.6) | copy-start | bytes 1769476
  2.6 25.9 %all-to-all-start = ((bf16[64,16,128]{2,1,0:T(8,128)(2,1)}), bf16[64,16,128]{2,1,0:T(8,128)(2,1)S(1)}, u32[]{:S(2)}, u32[]{:S(2)}) async-start(bf16[64,16,128]{2,1,0:T(8,128)(2,1)} %pad.13.clone), calls=%async_computation | async-start | bytes 524288 | tf_op jit(solution)/shard_map/all_to_all | solution.py:35
  18.4 2.3 %copy-start.3 = (bf16[6,64,2,128]{3,2,1,0:T(2,128)(2,1)}, bf16[6,64,2,128]{3,2,1,0:T(2,128)(2,1)S(1)}, u32[]{:S(2)}) copy-start(bf16[6,64,2,128]{3,2,1,0:T(2,128)(2,1)S(1)} %squeeze.12) | copy-start | bytes 589828
  18.5 11.9 %copy-start.5 = (bf16[6,64,2,128]{3,2,1,0:T(2,128)(2,1)}, bf16[6,64,2,128]{3,2,1,0:T(2,128)(2,1)S(1)}, u32[]{:S(2)}) copy-start(bf16[6,64,2,128]{3,2,1,0:T(2,128)(2,1)S(1)} %squeeze.13) | copy-start | bytes 589828
  18.5 11.9 %copy-start.1 = (bf16[6,64,2,128]{3,2,1,0:T(2,128)(2,1)}, bf16[6,64,2,128]{3,2,1,0:T(2,128)(2,1)S(1)}, u32[]{:S(2)}) copy-start(bf16[6,64,2,128]{3,2,1,0:T(2,128)(2,1)S(1)} %squeeze.14) | copy-start | bytes 589828
  28.5 7.4 %copy-start.7 = (f32[3200]{0:T(1024)S(1)}, f32[3200]{0:T(1024)}, u32[]{:S(2)}) copy-start(f32[3200]{0:T(1024)} %param.9) | copy-start | bytes 38404
  30.4 20.4 %all-to-all-start.1 = ((bf16[64,24,128]{2,1,0:T(8,128)(2,1)}), bf16[64,24,128]{2,1,0:T(8,128)(2,1)S(1)}, u32[]{:S(2)}, u32[]{:S(2)}) async-start(bf16[64,24,128]{2,1,0:T(8,128)(2,1)} %bitcast.2), calls=%async_computation.1 | async-start | bytes 786432 | tf_op jit(solution)/shard_map/all_to_all | solution.py:38
  51.3 44.3 %copy-start = (bf16[256,3200]{1,0:T(8,128)(2,1)S(1)}, bf16[256,3200]{1,0:T(8,128)(2,1)}, u32[]{:S(2)}) copy-start(bf16[256,3200]{1,0:T(8,128)(2,1)} %get-tuple-element.16.weight_ref) | copy-start | bytes 4915204
  51.3 19.2 %collective-permute-start.3 = (bf16[6,8,3200]{2,1,0:T(8,128)(2,1)S(1)}, bf16[6,8,3200]{2,1,0:T(8,128)(2,1)S(1)}, u32[]{:S(2)}, u32[]{:S(2)}) collective-permute-start(bf16[6,8,3200]{2,1,0:T(8,128)(2,1)S(1)} %reshape.492), channel_id=1, source_target_pairs={{0,4},{1,5},{2,6},{3,7},{4,0},{5,1},{6,2},{7,3},{8,12},{9,13},{10,... | collective-permute-start | bytes 921608 | tf_op jit(solution)/shard_map/ppermute | solution.py:49
  59.6 27.9 %collective-permute-start.2 = (bf16[6,8,3200]{2,1,0:T(8,128)(2,1)S(1)}, bf16[6,8,3200]{2,1,0:T(8,128)(2,1)S(1)}, u32[]{:S(2)}, u32[]{:S(2)}) collective-permute-start(bf16[6,8,3200]{2,1,0:T(8,128)(2,1)S(1)} %reshape.492), channel_id=1, source_target_pairs={{0,2},{1,3},{2,0},{3,1},{4,6},{5,7},{6,4},{7,5},{8,10},{9,11},{10,... | collective-permute-start | bytes 921608 | tf_op jit(solution)/shard_map/ppermute | solution.py:44
  64.6 22.9 %collective-permute-start.1 = (bf16[6,8,3200]{2,1,0:T(8,128)(2,1)S(1)}, bf16[6,8,3200]{2,1,0:T(8,128)(2,1)S(1)}, u32[]{:S(2)}, u32[]{:S(2)}) collective-permute-start(bf16[6,8,3200]{2,1,0:T(8,128)(2,1)S(1)} %reshape.492), channel_id=1, source_target_pairs={{0,3},{1,0},{2,1},{3,2},{4,7},{5,4},{6,5},{7,6},{8,11},{9,8},{10,9... | collective-permute-start | bytes 921608 | tf_op jit(solution)/shard_map/ppermute | solution.py:44
  67.6 17.9 %collective-permute-start = (bf16[6,8,3200]{2,1,0:T(8,128)(2,1)S(1)}, bf16[6,8,3200]{2,1,0:T(8,128)(2,1)S(1)}, u32[]{:S(2)}, u32[]{:S(2)}) collective-permute-start(bf16[6,8,3200]{2,1,0:T(8,128)(2,1)S(1)} %reshape.492), channel_id=1, source_target_pairs={{0,1},{1,2},{2,3},{3,0},{4,5},{5,6},{6,7},{7,4},{8,9},{9,10},{10,1... | collective-permute-start | bytes 921608 | tf_op jit(solution)/shard_map/ppermute | solution.py:44
  70.5 25.1 %collective-permute-start.6 = (bf16[6,8,3200]{2,1,0:T(8,128)(2,1)S(1)}, bf16[6,8,3200]{2,1,0:T(8,128)(2,1)S(1)}, u32[]{:S(2)}, u32[]{:S(2)}) collective-permute-start(bf16[6,8,3200]{2,1,0:T(8,128)(2,1)S(1)} %collective-permute-done.3), channel_id=1, source_target_pairs={{0,2},{1,3},{2,0},{3,1},{4,6},{5,7},{6,4},{7,5},{8,10},{9,11},{10,... | collective-permute-start | bytes 921608 | tf_op jit(solution)/shard_map/ppermute | solution.py:44
  73.0 22.5 %collective-permute-start.5 = (bf16[6,8,3200]{2,1,0:T(8,128)(2,1)S(1)}, bf16[6,8,3200]{2,1,0:T(8,128)(2,1)S(1)}, u32[]{:S(2)}, u32[]{:S(2)}) collective-permute-start(bf16[6,8,3200]{2,1,0:T(8,128)(2,1)S(1)} %collective-permute-done.3), channel_id=1, source_target_pairs={{0,3},{1,0},{2,1},{3,2},{4,7},{5,4},{6,5},{7,6},{8,11},{9,8},{10,9... | collective-permute-start | bytes 921608 | tf_op jit(solution)/shard_map/ppermute | solution.py:44
  85.5 9.9 %collective-permute-start.4 = (bf16[6,8,3200]{2,1,0:T(8,128)(2,1)S(1)}, bf16[6,8,3200]{2,1,0:T(8,128)(2,1)S(1)}, u32[]{:S(2)}, u32[]{:S(2)}) collective-permute-start(bf16[6,8,3200]{2,1,0:T(8,128)(2,1)S(1)} %collective-permute-done.3), channel_id=1, source_target_pairs={{0,1},{1,2},{2,3},{3,0},{4,5},{5,6},{6,7},{7,4},{8,9},{9,10},{10,1... | collective-permute-start | bytes 921608 | tf_op jit(solution)/shard_map/ppermute | solution.py:44
  98.9 17.7 %collective-permute-start.7 = (bf16[128,3200]{1,0:T(8,128)(2,1)}, bf16[128,3200]{1,0:T(8,128)(2,1)}, u32[]{:S(2)}, u32[]{:S(2)}) collective-permute-start(bf16[128,3200]{1,0:T(8,128)(2,1)} %get-tuple-element.8), channel_id=1, source_target_pairs={{0,8},{8,0},{16,24},{24,16},{32,40},{40,32},{48,56},{56,48},{64,72... | collective-permute-start | bytes 2457608 | tf_op jit(solution)/shard_map/ppermute | solution.py:197
  120.0 39.0 %all-to-all-start.3 = ((bf16[32,4,4096]{2,1,0:T(4,128)(2,1)}), bf16[32,4,4096]{2,1,0:T(4,128)(2,1)S(1)}, u32[]{:S(2)}, u32[]{:S(2)}) async-start(bf16[32,4,4096]{2,1,0:T(4,128)(2,1)} %outgoing_blocks.1), calls=%async_computation.3 | async-start | bytes 2097152 | tf_op jit(solution)/shard_map/all_to_all | solution.py:205
  133.7 4.6 %copy-start.6 = (bf16[6,64,2,128]{3,2,1,0:T(2,128)(2,1)S(1)}, bf16[6,64,2,128]{3,2,1,0:T(2,128)(2,1)}, u32[]{:S(2)}) copy-start(bf16[6,64,2,128]{3,2,1,0:T(2,128)(2,1)} %copy-done.5) | copy-start | bytes 589828
  137.9 2.2 %copy-start.4 = (bf16[6,64,2,128]{3,2,1,0:T(2,128)(2,1)S(1)}, bf16[6,64,2,128]{3,2,1,0:T(2,128)(2,1)}, u32[]{:S(2)}) copy-start(bf16[6,64,2,128]{3,2,1,0:T(2,128)(2,1)} %copy-done.3) | copy-start | bytes 589828

commit v4 on v3

--- a/solution.py
+++ b/solution.py
@@ -119,16 +119,20 @@
 def outgoing_body(kept_ref, taken_ref, extra_ref, out_ref):
     width = kept_ref.shape[1]
     held = out_ref.shape[1]
-    total = kept_ref[...].astype(jnp.float32) + taken_ref[...].astype(jnp.float32)
+    for begin in range(0, width, 640):
+        columns = slice(begin, begin + 640)
+        total = kept_ref[:, columns].astype(jnp.float32) + taken_ref[:, columns].astype(jnp.float32)
+        for block in range(out_ref.shape[0]):
+            rows = total[block * held : (block + 1) * held]
+            out_ref[block, :, columns] = rows.astype(jnp.bfloat16)
     for block in range(out_ref.shape[0]):
-        out_ref[block, :, :width] = total[block * held : (block + 1) * held].astype(jnp.bfloat16)
         out_ref[block, :, width:] = extra_ref[...]
 
 
 def outgoing_blocks(kept, taken, extra):
     rows, width = kept.shape
     held, more = extra.shape
-    step = 32
+    step = 64
     by_row = pl.BlockSpec((step, width), lambda i: (i, 0))
     return pl.pallas_call(
         outgoing_body,

time: 162 us -> 160 us (0.988)
  transfers between devices with their start and end apart: 11 -> 11, of which waited for: 5 -> 5; matrix products, arithmetic and copies ran while one was open for 15% -> 16% of each run, Pallas kernels for 0% -> 0%
where the time goes in v4:
time: 160 us
  starting transfers between devices  58.9 us (37%)
  waiting for transfers between devices  48.5 us (30%)
  matrix products  14.6 us (9%)
  blocking collectives  14.4 us (9%)
  local copies, waits for them, and re-layouts  12.1 us (8%)
  Pallas kernels  5.47 us (3%)
  other arithmetic  4.32 us (3%)
    ppermute x6, starting transfers between devices, ring_gather(): lax.ppermute(block, 'tensor', tensor_step(0, k))  19.8 us
    all_to_all x1, waiting for transfers between devices, local(): lax.all_to_all(outgoing, 'replica', 0, 0, axis_index_groups=columns)  17.3 us
    ppermute x6, waiting for transfers between devices, ring_gather(): lax.ppermute(block, 'tensor', tensor_step(0, k))  15.8 us
    all_to_all x1, blocking collectives, over_chip_and_tensor(): lax.all_to_all(copies, ('replica', 'tensor'), 0, 0, axis_index_groups=near)  14.4 us
    all_to_all x1, starting transfers between devices, deal(): lax.all_to_all(spread, 'replica', 0, 0)  13.5 us
    all_to_all x1, starting transfers between devices, local(): lax.all_to_all(outgoing, 'replica', 0, 0, axis_index_groups=columns)  9.98 us
    ppermute x1, starting transfers between devices, gather_tokens(): other = lax.ppermute(block, 'tensor', tensor_step(1, 0))  8.35 us
    all_to_all x1, waiting for transfers between devices, deal(): lax.all_to_all(spread, 'replica', 0, 0)  7.77 us
  transfers between devices with their start and end apart: 11, of which 5 were waited for; matrix products, arithmetic and copies ran while one was open for 16% of the time, Pallas kernels for 0%

profile of v4, /device:TPU:8, one launch (start us, length us, event | category | flops | bytes accessed | tf_op | source)
XLA Modules:
  0.0 159.6 jit_solution(4773951079244200044)
XLA Ops:
  2.6 13.5 %all-to-all-start = ((bf16[64,16,128]{2,1,0:T(8,128)(2,1)}), bf16[64,16,128]{2,1,0:T(8,128)(2,1)S(1)}, u32[]{:S(2)}, u32[]{:S(2)}) async-start(bf16[64,16,128]{2,1,0:T(8,128)(2,1)} %pad.13.clone), calls=%async_computation | async-start | bytes 524288 | tf_op jit(solution)/shard_map/all_to_all | solution.py:35
  20.7 7.8 %all-to-all-done = bf16[64,16,128]{2,1,0:T(8,128)(2,1)S(1)} async-done(((bf16[64,16,128]{2,1,0:T(8,128)(2,1)}), bf16[64,16,128]{2,1,0:T(8,128)(2,1)S(1)}, u32[]{:S(2)}, u32[]{:S(2)}) %all-to-all-start) | async-done | bytes 262176 | tf_op jit(solution)/shard_map/all_to_all | solution.py:35
  28.5 1.9 %fusion.4 = bf16[1536,128]{1,0:T(8,128)(2,1)} fusion(bf16[1024,128]{1,0:T(8,128)(2,1)S(1)} %bitcast.84, s32[1024]{0:T(1024)S(1)} %add.216), kind=kOutput, calls=%fused_computation.8 | convolution fusion | flops 404422656 | bytes 659456 | tf_op jit(solution)/shard_map/mi,ic->mc/dot_general | solution.py:36
  30.4 5.4 %all-to-all-start.1 = ((bf16[64,24,128]{2,1,0:T(8,128)(2,1)}), bf16[64,24,128]{2,1,0:T(8,128)(2,1)S(1)}, u32[]{:S(2)}, u32[]{:S(2)}) async-start(bf16[64,24,128]{2,1,0:T(8,128)(2,1)} %bitcast.2), calls=%async_computation.1 | async-start | bytes 786432 | tf_op jit(solution)/shard_map/all_to_all | solution.py:38
  36.7 3.7 %reshape.497 = bf16[256,3200]{1,0:T(8,128)(2,1)S(1)} reshape(bf16[128,2,3200]{2,1,0:T(2,128)(2,1)} %param.8) | data formatting | bytes 3276800 | tf_op jit(solution)/shard_map/reshape | solution.py:183
  40.4 2.9 %fusion.83 = (bf16[256,3200]{1,0:T(8,128)(2,1)}, f32[256,3200]{1,0:T(8,128)}) fusion(bf16[256,3200]{1,0:T(8,128)(2,1)S(1)} %reshape.497, s32[256]{0:T(256)S(1)} %get-tuple-element.18), kind=kOutput, calls=%fused_computation.104 | convolution fusion | flops 420315136 | bytes 6554624 | tf_op jit(solution)/shard_map/wp,wc->pc/dot_general | solution.py:180
  43.3 7.5 %all-to-all-done.1 = bf16[64,24,128]{2,1,0:T(8,128)(2,1)S(1)} async-done(((bf16[64,24,128]{2,1,0:T(8,128)(2,1)}), bf16[64,24,128]{2,1,0:T(8,128)(2,1)S(1)}, u32[]{:S(2)}, u32[]{:S(2)}) %all-to-all-start.1) | async-done | bytes 393248 | tf_op jit(solution)/shard_map/all_to_all | solution.py:38
  51.3 8.4 %collective-permute-start.3 = (bf16[6,8,3200]{2,1,0:T(8,128)(2,1)S(1)}, bf16[6,8,3200]{2,1,0:T(8,128)(2,1)S(1)}, u32[]{:S(2)}, u32[]{:S(2)}) collective-permute-start(bf16[6,8,3200]{2,1,0:T(8,128)(2,1)S(1)} %reshape.492), channel_id=1, source_target_pairs={{0,4},{1,5},{2,6},{3,7},{4,0},{5,1},{6,2},{7,3},{8,12},{9,13},{10,... | collective-permute-start | bytes 921608 | tf_op jit(solution)/shard_map/ppermute | solution.py:49
  59.6 4.9 %collective-permute-start.2 = (bf16[6,8,3200]{2,1,0:T(8,128)(2,1)S(1)}, bf16[6,8,3200]{2,1,0:T(8,128)(2,1)S(1)}, u32[]{:S(2)}, u32[]{:S(2)}) collective-permute-start(bf16[6,8,3200]{2,1,0:T(8,128)(2,1)S(1)} %reshape.492), channel_id=1, source_target_pairs={{0,2},{1,3},{2,0},{3,1},{4,6},{5,7},{6,4},{7,5},{8,10},{9,11},{10,... | collective-permute-start | bytes 921608 | tf_op jit(solution)/shard_map/ppermute | solution.py:44
  64.6 3.0 %collective-permute-start.1 = (bf16[6,8,3200]{2,1,0:T(8,128)(2,1)S(1)}, bf16[6,8,3200]{2,1,0:T(8,128)(2,1)S(1)}, u32[]{:S(2)}, u32[]{:S(2)}) collective-permute-start(bf16[6,8,3200]{2,1,0:T(8,128)(2,1)S(1)} %reshape.492), channel_id=1, source_target_pairs={{0,3},{1,0},{2,1},{3,2},{4,7},{5,4},{6,5},{7,6},{8,11},{9,8},{10,9... | collective-permute-start | bytes 921608 | tf_op jit(solution)/shard_map/ppermute | solution.py:44
  67.6 2.8 %collective-permute-start = (bf16[6,8,3200]{2,1,0:T(8,128)(2,1)S(1)}, bf16[6,8,3200]{2,1,0:T(8,128)(2,1)S(1)}, u32[]{:S(2)}, u32[]{:S(2)}) collective-permute-start(bf16[6,8,3200]{2,1,0:T(8,128)(2,1)S(1)} %reshape.492), channel_id=1, source_target_pairs={{0,1},{1,2},{2,3},{3,0},{4,5},{5,6},{6,7},{7,4},{8,9},{9,10},{10,1... | collective-permute-start | bytes 921608 | tf_op jit(solution)/shard_map/ppermute | solution.py:44
  70.5 2.6 %collective-permute-start.6 = (bf16[6,8,3200]{2,1,0:T(8,128)(2,1)S(1)}, bf16[6,8,3200]{2,1,0:T(8,128)(2,1)S(1)}, u32[]{:S(2)}, u32[]{:S(2)}) collective-permute-start(bf16[6,8,3200]{2,1,0:T(8,128)(2,1)S(1)} %collective-permute-done.3), channel_id=1, source_target_pairs={{0,2},{1,3},{2,0},{3,1},{4,6},{5,7},{6,4},{7,5},{8,10},{9,11},{10,... | collective-permute-start | bytes 921608 | tf_op jit(solution)/shard_map/ppermute | solution.py:44
  73.0 4.5 %collective-permute-start.5 = (bf16[6,8,3200]{2,1,0:T(8,128)(2,1)S(1)}, bf16[6,8,3200]{2,1,0:T(8,128)(2,1)S(1)}, u32[]{:S(2)}, u32[]{:S(2)}) collective-permute-start(bf16[6,8,3200]{2,1,0:T(8,128)(2,1)S(1)} %collective-permute-done.3), channel_id=1, source_target_pairs={{0,3},{1,0},{2,1},{3,2},{4,7},{5,4},{6,5},{7,6},{8,11},{9,8},{10,9... | collective-permute-start | bytes 921608 | tf_op jit(solution)/shard_map/ppermute | solution.py:44
  77.6 8.0 %collective-permute-done = bf16[6,8,3200]{2,1,0:T(8,128)(2,1)S(1)} collective-permute-done((bf16[6,8,3200]{2,1,0:T(8,128)(2,1)S(1)}, bf16[6,8,3200]{2,1,0:T(8,128)(2,1)S(1)}, u32[]{:S(2)}, u32[]{:S(2)}) %collective-permute-start) | collective-permute-done | bytes 307232 | tf_op jit(solution)/shard_map/ppermute | solution.py:44
  85.5 1.9 %collective-permute-start.4 = (bf16[6,8,3200]{2,1,0:T(8,128)(2,1)S(1)}, bf16[6,8,3200]{2,1,0:T(8,128)(2,1)S(1)}, u32[]{:S(2)}, u32[]{:S(2)}) collective-permute-start(bf16[6,8,3200]{2,1,0:T(8,128)(2,1)S(1)} %collective-permute-done.3), channel_id=1, source_target_pairs={{0,1},{1,2},{2,3},{3,0},{4,5},{5,6},{6,7},{7,4},{8,9},{9,10},{10,1... | collective-permute-start | bytes 921608 | tf_op jit(solution)/shard_map/ppermute | solution.py:44
  87.6 7.9 %collective-permute-done.4 = bf16[6,8,3200]{2,1,0:T(8,128)(2,1)S(1)} collective-permute-done((bf16[6,8,3200]{2,1,0:T(8,128)(2,1)S(1)}, bf16[6,8,3200]{2,1,0:T(8,128)(2,1)S(1)}, u32[]{:S(2)}, u32[]{:S(2)}) %collective-permute-start.4) | collective-permute-done | bytes 307232 | tf_op jit(solution)/shard_map/ppermute | solution.py:44
  95.6 3.3 %weight_products.1 = (bf16[128,3200]{1,0:T(8,128)(2,1)}, bf16[128,3200]{1,0:T(8,128)(2,1)S(1)}, f32[1,3200]{1,0:T(1,128)S(1)}) custom-call(bf16[256,384]{1,0:T(8,128)(2,1)S(1)} %bitcast.77, bf16[384,3200]{1,0:T(8,128)(2,1)S(1)} %bitcast.75, bf16[256,3200]{1,0:T(8,128)(2,1)S(1)} %copy-done, f32[1,3200]{1,0:T(1,128)S(1)} %broadcast_in_dim.22.gain_ref), custom_call_target="tpu_custom_call" | custom-call | flops 629145600 | bytes 7340032 | tf_op jit(solution)/shard_map/weight_products/pallas_call | solution.py:96
  98.9 1.9 %collective-permute-start.7 = (bf16[128,3200]{1,0:T(8,128)(2,1)}, bf16[128,3200]{1,0:T(8,128)(2,1)}, u32[]{:S(2)}, u32[]{:S(2)}) collective-permute-start(bf16[128,3200]{1,0:T(8,128)(2,1)} %get-tuple-element.8), channel_id=1, source_target_pairs={{0,8},{8,0},{16,24},{24,16},{32,40},{40,32},{48,56},{56,48},{64,72... | collective-permute-start | bytes 2457608 | tf_op jit(solution)/shard_map/ppermute | solution.py:201
  101.0 14.4 %all_to_all.20 = f32[16,1,3200]{2,1,0:T(1,128)} all-to-all(f32[16,1,3200]{2,1,0:T(1,128)S(1)} %broadcast_in_dim.23), channel_id=1, replica_groups={{0,1,2,3,4,5,6,7,8,9,10,11,12,13,14,15},{16,17,18,19,20,21,22,23,24,25,..., dimensions={0} | all-to-all | bytes 409600 | tf_op jit(solution)/shard_map/all_to_all | solution.py:76
  116.6 2.1 %outgoing_blocks.1 = bf16[32,4,4096]{2,1,0:T(4,128)(2,1)} custom-call(bf16[128,3200]{1,0:T(8,128)(2,1)S(1)} %get-tuple-element.7.kept_ref, bf16[128,3200]{1,0:T(8,128)(2,1)} %collective-permute-done.7.taken_ref, bf16[4,896]{1,0:T(4,128)(2,1)S(1)} %pad.14.extra_ref), custom_call_target="tpu_custom_call" | custom-call | flops 409600 | bytes 4194304 | tf_op jit(solution)/shard_map/outgoing_blocks/pallas_call | solution.py:137
  118.8 10.0 %all-to-all-start.3 = ((bf16[32,4,4096]{2,1,0:T(4,128)(2,1)}), bf16[32,4,4096]{2,1,0:T(4,128)(2,1)S(1)}, u32[]{:S(2)}, u32[]{:S(2)}) async-start(bf16[32,4,4096]{2,1,0:T(4,128)(2,1)} %outgoing_blocks.1), calls=%async_computation.3 | async-start | bytes 2097152 | tf_op jit(solution)/shard_map/all_to_all | solution.py:209
  128.8 3.6 %convolution_convert_fusion.3 = bf16[384,256]{1,0:T(8,128)(2,1)} fusion(bf16[384,3200]{1,0:T(8,128)(2,1)S(1)} %bitcast.76, f32[256,3200]{1,0:T(8,128)} %get-tuple-element.17, f32[3200]{0:T(1024)S(1)} %copy-done.7, s32[256]{0:T(256)S(1)} %get-tuple-element.19), kind=kOutput, calls=%fused_computation.23 | convolution fusion | flops 681377792 | bytes 5944832 | tf_op jit(solution)/shard_map/np,wp->nw/dot_general | solution.py:218
  132.4 1.5 gather_fusion.1
  140.4 17.3 %all-to-all-done.3 = bf16[32,4,4096]{2,1,0:T(4,128)(2,1)S(1)} async-done(((bf16[32,4,4096]{2,1,0:T(4,128)(2,1)}), bf16[32,4,4096]{2,1,0:T(4,128)(2,1)S(1)}, u32[]{:S(2)}, u32[]{:S(2)}) %all-to-all-start.3) | async-done | bytes 1048608 | tf_op jit(solution)/shard_map/all_to_all | solution.py:209
  (86 shorter events, 17.4 us)
Async XLA Ops:
  0.6 17.6 %copy-start.2 = (bf16[3,6,64,256]{3,2,1,0:T(8,128)(2,1)S(1)}, bf16[3,6,64,256]{3,2,1,0:T(8,128)(2,1)}, u32[]{:S(2)}) copy-start(bf16[3,6,64,256]{3,2,1,0:T(8,128)(2,1)} %param.6) | copy-start | bytes 1769476
  2.6 25.9 %all-to-all-start = ((bf16[64,16,128]{2,1,0:T(8,128)(2,1)}), bf16[64,16,128]{2,1,0:T(8,128)(2,1)S(1)}, u32[]{:S(2)}, u32[]{:S(2)}) async-start(bf16[64,16,128]{2,1,0:T(8,128)(2,1)} %pad.13.clone), calls=%async_computation | async-start | bytes 524288 | tf_op jit(solution)/shard_map/all_to_all | solution.py:35
  18.4 2.3 %copy-start.3 = (bf16[6,64,2,128]{3,2,1,0:T(2,128)(2,1)}, bf16[6,64,2,128]{3,2,1,0:T(2,128)(2,1)S(1)}, u32[]{:S(2)}) copy-start(bf16[6,64,2,128]{3,2,1,0:T(2,128)(2,1)S(1)} %squeeze.12) | copy-start | bytes 589828
  18.5 11.9 %copy-start.5 = (bf16[6,64,2,128]{3,2,1,0:T(2,128)(2,1)}, bf16[6,64,2,128]{3,2,1,0:T(2,128)(2,1)S(1)}, u32[]{:S(2)}) copy-start(bf16[6,64,2,128]{3,2,1,0:T(2,128)(2,1)S(1)} %squeeze.13) | copy-start | bytes 589828
  18.5 11.9 %copy-start.1 = (bf16[6,64,2,128]{3,2,1,0:T(2,128)(2,1)}, bf16[6,64,2,128]{3,2,1,0:T(2,128)(2,1)S(1)}, u32[]{:S(2)}) copy-start(bf16[6,64,2,128]{3,2,1,0:T(2,128)(2,1)S(1)} %squeeze.14) | copy-start | bytes 589828
  28.5 7.4 %copy-start.7 = (f32[3200]{0:T(1024)S(1)}, f32[3200]{0:T(1024)}, u32[]{:S(2)}) copy-start(f32[3200]{0:T(1024)} %param.9) | copy-start | bytes 38404
  30.4 20.4 %all-to-all-start.1 = ((bf16[64,24,128]{2,1,0:T(8,128)(2,1)}), bf16[64,24,128]{2,1,0:T(8,128)(2,1)S(1)}, u32[]{:S(2)}, u32[]{:S(2)}) async-start(bf16[64,24,128]{2,1,0:T(8,128)(2,1)} %bitcast.2), calls=%async_computation.1 | async-start | bytes 786432 | tf_op jit(solution)/shard_map/all_to_all | solution.py:38
  51.3 44.3 %copy-start = (bf16[256,3200]{1,0:T(8,128)(2,1)S(1)}, bf16[256,3200]{1,0:T(8,128)(2,1)}, u32[]{:S(2)}) copy-start(bf16[256,3200]{1,0:T(8,128)(2,1)} %get-tuple-element.16.weight_ref) | copy-start | bytes 4915204
  51.3 19.2 %collective-permute-start.3 = (bf16[6,8,3200]{2,1,0:T(8,128)(2,1)S(1)}, bf16[6,8,3200]{2,1,0:T(8,128)(2,1)S(1)}, u32[]{:S(2)}, u32[]{:S(2)}) collective-permute-start(bf16[6,8,3200]{2,1,0:T(8,128)(2,1)S(1)} %reshape.492), channel_id=1, source_target_pairs={{0,4},{1,5},{2,6},{3,7},{4,0},{5,1},{6,2},{7,3},{8,12},{9,13},{10,... | collective-permute-start | bytes 921608 | tf_op jit(solution)/shard_map/ppermute | solution.py:49
  59.6 27.9 %collective-permute-start.2 = (bf16[6,8,3200]{2,1,0:T(8,128)(2,1)S(1)}, bf16[6,8,3200]{2,1,0:T(8,128)(2,1)S(1)}, u32[]{:S(2)}, u32[]{:S(2)}) collective-permute-start(bf16[6,8,3200]{2,1,0:T(8,128)(2,1)S(1)} %reshape.492), channel_id=1, source_target_pairs={{0,2},{1,3},{2,0},{3,1},{4,6},{5,7},{6,4},{7,5},{8,10},{9,11},{10,... | collective-permute-start | bytes 921608 | tf_op jit(solution)/shard_map/ppermute | solution.py:44
  64.6 22.9 %collective-permute-start.1 = (bf16[6,8,3200]{2,1,0:T(8,128)(2,1)S(1)}, bf16[6,8,3200]{2,1,0:T(8,128)(2,1)S(1)}, u32[]{:S(2)}, u32[]{:S(2)}) collective-permute-start(bf16[6,8,3200]{2,1,0:T(8,128)(2,1)S(1)} %reshape.492), channel_id=1, source_target_pairs={{0,3},{1,0},{2,1},{3,2},{4,7},{5,4},{6,5},{7,6},{8,11},{9,8},{10,9... | collective-permute-start | bytes 921608 | tf_op jit(solution)/shard_map/ppermute | solution.py:44
  67.6 17.9 %collective-permute-start = (bf16[6,8,3200]{2,1,0:T(8,128)(2,1)S(1)}, bf16[6,8,3200]{2,1,0:T(8,128)(2,1)S(1)}, u32[]{:S(2)}, u32[]{:S(2)}) collective-permute-start(bf16[6,8,3200]{2,1,0:T(8,128)(2,1)S(1)} %reshape.492), channel_id=1, source_target_pairs={{0,1},{1,2},{2,3},{3,0},{4,5},{5,6},{6,7},{7,4},{8,9},{9,10},{10,1... | collective-permute-start | bytes 921608 | tf_op jit(solution)/shard_map/ppermute | solution.py:44
  70.5 25.1 %collective-permute-start.6 = (bf16[6,8,3200]{2,1,0:T(8,128)(2,1)S(1)}, bf16[6,8,3200]{2,1,0:T(8,128)(2,1)S(1)}, u32[]{:S(2)}, u32[]{:S(2)}) collective-permute-start(bf16[6,8,3200]{2,1,0:T(8,128)(2,1)S(1)} %collective-permute-done.3), channel_id=1, source_target_pairs={{0,2},{1,3},{2,0},{3,1},{4,6},{5,7},{6,4},{7,5},{8,10},{9,11},{10,... | collective-permute-start | bytes 921608 | tf_op jit(solution)/shard_map/ppermute | solution.py:44
  73.0 22.5 %collective-permute-start.5 = (bf16[6,8,3200]{2,1,0:T(8,128)(2,1)S(1)}, bf16[6,8,3200]{2,1,0:T(8,128)(2,1)S(1)}, u32[]{:S(2)}, u32[]{:S(2)}) collective-permute-start(bf16[6,8,3200]{2,1,0:T(8,128)(2,1)S(1)} %collective-permute-done.3), channel_id=1, source_target_pairs={{0,3},{1,0},{2,1},{3,2},{4,7},{5,4},{6,5},{7,6},{8,11},{9,8},{10,9... | collective-permute-start | bytes 921608 | tf_op jit(solution)/shard_map/ppermute | solution.py:44
  85.5 9.9 %collective-permute-start.4 = (bf16[6,8,3200]{2,1,0:T(8,128)(2,1)S(1)}, bf16[6,8,3200]{2,1,0:T(8,128)(2,1)S(1)}, u32[]{:S(2)}, u32[]{:S(2)}) collective-permute-start(bf16[6,8,3200]{2,1,0:T(8,128)(2,1)S(1)} %collective-permute-done.3), channel_id=1, source_target_pairs={{0,1},{1,2},{2,3},{3,0},{4,5},{5,6},{6,7},{7,4},{8,9},{9,10},{10,1... | collective-permute-start | bytes 921608 | tf_op jit(solution)/shard_map/ppermute | solution.py:44
  98.9 17.7 %collective-permute-start.7 = (bf16[128,3200]{1,0:T(8,128)(2,1)}, bf16[128,3200]{1,0:T(8,128)(2,1)}, u32[]{:S(2)}, u32[]{:S(2)}) collective-permute-start(bf16[128,3200]{1,0:T(8,128)(2,1)} %get-tuple-element.8), channel_id=1, source_target_pairs={{0,8},{8,0},{16,24},{24,16},{32,40},{40,32},{48,56},{56,48},{64,72... | collective-permute-start | bytes 2457608 | tf_op jit(solution)/shard_map/ppermute | solution.py:201
  118.8 39.0 %all-to-all-start.3 = ((bf16[32,4,4096]{2,1,0:T(4,128)(2,1)}), bf16[32,4,4096]{2,1,0:T(4,128)(2,1)S(1)}, u32[]{:S(2)}, u32[]{:S(2)}) async-start(bf16[32,4,4096]{2,1,0:T(4,128)(2,1)} %outgoing_blocks.1), calls=%async_computation.3 | async-start | bytes 2097152 | tf_op jit(solution)/shard_map/all_to_all | solution.py:209
  132.4 4.6 %copy-start.6 = (bf16[6,64,2,128]{3,2,1,0:T(2,128)(2,1)S(1)}, bf16[6,64,2,128]{3,2,1,0:T(2,128)(2,1)}, u32[]{:S(2)}) copy-start(bf16[6,64,2,128]{3,2,1,0:T(2,128)(2,1)} %copy-done.5) | copy-start | bytes 589828
  136.6 2.2 %copy-start.4 = (bf16[6,64,2,128]{3,2,1,0:T(2,128)(2,1)S(1)}, bf16[6,64,2,128]{3,2,1,0:T(2,128)(2,1)}, u32[]{:S(2)}) copy-start(bf16[6,64,2,128]{3,2,1,0:T(2,128)(2,1)} %copy-done.3) | copy-start | bytes 589828

commit v5 on v4

--- a/solution.py
+++ b/solution.py
@@ -73,8 +73,7 @@
         for chip in range(32)
     ]
     copies = jnp.broadcast_to(part, (16, 1) + part.shape)
-    arrived = lax.all_to_all(copies, ("replica", "tensor"), 0, 0, axis_index_groups=near)
-    return jnp.sum(arrived, axis=(0, 1))
+    return lax.all_to_all(copies, ("replica", "tensor"), 0, 0, axis_index_groups=near)
 
 
 def product_body(left_ref, right_ref, weight_ref, gain_ref, given_ref, kept_ref, scale_ref):
@@ -116,28 +115,34 @@
     )(left, right, weights, gain)
 
 
-def outgoing_body(kept_ref, taken_ref, extra_ref, out_ref):
+def outgoing_body(kept_ref, taken_ref, terms_ref, out_ref):
     width = kept_ref.shape[1]
     held = out_ref.shape[1]
+    more = out_ref.shape[2] - width
     for begin in range(0, width, 640):
         columns = slice(begin, begin + 640)
         total = kept_ref[:, columns].astype(jnp.float32) + taken_ref[:, columns].astype(jnp.float32)
         for block in range(out_ref.shape[0]):
             rows = total[block * held : (block + 1) * held]
             out_ref[block, :, columns] = rows.astype(jnp.bfloat16)
+    terms = jnp.sum(terms_ref[...], axis=0)
+    rows = [terms[:, row * more : min((row + 1) * more, width)] for row in range(held)]
+    empty = jnp.zeros((1, held * more - width), jnp.float32)
+    rows[-1] = jnp.concatenate([rows[-1], empty], axis=1)
+    extra = jnp.concatenate(rows).astype(jnp.bfloat16)
     for block in range(out_ref.shape[0]):
-        out_ref[block, :, width:] = extra_ref[...]
-
-
-def outgoing_blocks(kept, taken, extra):
+        out_ref[block, :, width:] = extra
+
+
+def outgoing_blocks(kept, taken, terms, held):
     rows, width = kept.shape
-    held, more = extra.shape
+    more = -(-width // (held * 128)) * 128
     step = 64
     by_row = pl.BlockSpec((step, width), lambda i: (i, 0))
     return pl.pallas_call(
         outgoing_body,
         grid=(rows // step,),
-        in_specs=[by_row, by_row, pl.BlockSpec((held, more), lambda i: (0, 0))],
+        in_specs=[by_row, by_row, pl.BlockSpec(terms.shape, lambda i: (0, 0, 0))],
         out_specs=pl.BlockSpec((step // held, held, width + more), lambda i: (i, 0, 0)),
         out_shape=jax.ShapeDtypeStruct((rows // held, held, width + more), jnp.bfloat16),
         compiler_params=pltpu.CompilerParams(vmem_limit_bytes=24 * 2**20),
@@ -145,7 +150,7 @@
             flops=rows * width, bytes_accessed=4 * 2**20, transcendentals=0
         ),
         name="outgoing_blocks",
-    )(kept, taken, extra)
+    )(kept, taken, terms)
 
 
 def local(owner, qkv, grad_out, w_out, layer_scale):
@@ -203,13 +208,11 @@
         [z * 16 + y * 2 + c for z in range(4) for y in range(8)] for c in range(2)
     ]
     held = rows // 64
-    extra = over_chip_and_tensor(scale_part[0]).astype(jnp.bfloat16)
-    extra = jnp.pad(extra.reshape(held, width // held), ((0, 0), (0, 96)))
-    outgoing = outgoing_blocks(kept, taken, extra)
+    outgoing = outgoing_blocks(kept, taken, over_chip_and_tensor(scale_part[0]), held)
     arrived = lax.all_to_all(outgoing, "replica", 0, 0, axis_index_groups=columns)
     summed = jnp.sum(arrived.astype(jnp.float32), axis=0)
     grad_w = summed[:, :width].reshape(size // 64, heads, width)
-    grad_scale = summed[:, width : width + width // held].reshape(width)
+    grad_scale = summed[:, width:].reshape(-1)[:width]
 
     flat, _ = lax.optimization_barrier((flat, outgoing))
     d_flat = jnp.einsum(

time: 160 us -> 159 us (level)
  transfers between devices with their start and end apart: 11 -> 11, of which waited for: 5 -> 5; matrix products, arithmetic and copies ran while one was open for 16% -> 15% of each run, Pallas kernels for 0% -> 0%
where the time goes in v5:
time: 159 us; the launch traced here: 158 us
  starting transfers between devices  58.9 us (37%)
  waiting for transfers between devices  48.5 us (31%)
  matrix products  14.6 us (9%)
  blocking collectives  13.8 us (9%)
  local copies, waits for them, and re-layouts  12 us (8%)
  Pallas kernels  5.65 us (4%)
  other arithmetic  3.25 us (2%)
    ppermute x6, starting transfers between devices, ring_gather(): lax.ppermute(block, 'tensor', tensor_step(0, k))  19.8 us
    all_to_all x1, waiting for transfers between devices, local(): lax.all_to_all(outgoing, 'replica', 0, 0, axis_index_groups=columns)  17.3 us
    ppermute x6, waiting for transfers between devices, ring_gather(): lax.ppermute(block, 'tensor', tensor_step(0, k))  15.8 us
    all_to_all x1, blocking collectives, over_chip_and_tensor(): lax.all_to_all(copies, ('replica', 'tensor'), 0, 0, axis_index_groups=near)  13.8 us
    all_to_all x1, starting transfers between devices, deal(): lax.all_to_all(spread, 'replica', 0, 0)  13.5 us
    all_to_all x1, starting transfers between devices, local(): lax.all_to_all(outgoing, 'replica', 0, 0, axis_index_groups=columns)  9.98 us
    ppermute x1, starting transfers between devices, gather_tokens(): other = lax.ppermute(block, 'tensor', tensor_step(1, 0))  8.35 us
    all_to_all x1, waiting for transfers between devices, deal(): lax.all_to_all(spread, 'replica', 0, 0)  7.77 us
  transfers between devices with their start and end apart: 11, of which 5 were waited for; matrix products, arithmetic and copies ran while one was open for 15% of the time, Pallas kernels for 0%

profile of v5, /device:TPU:8, one launch (start us, length us, event | category | flops | bytes accessed | tf_op | source)
XLA Modules:
  0.0 157.8 jit_solution(12075459632888472915)
XLA Ops:
  2.6 13.5 %all-to-all-start = ((bf16[64,16,128]{2,1,0:T(8,128)(2,1)}), bf16[64,16,128]{2,1,0:T(8,128)(2,1)S(1)}, u32[]{:S(2)}, u32[]{:S(2)}) async-start(bf16[64,16,128]{2,1,0:T(8,128)(2,1)} %pad.9.clone), calls=%async_computation | async-start | bytes 524288 | tf_op jit(solution)/shard_map/all_to_all | solution.py:35
  20.7 7.8 %all-to-all-done = bf16[64,16,128]{2,1,0:T(8,128)(2,1)S(1)} async-done(((bf16[64,16,128]{2,1,0:T(8,128)(2,1)}), bf16[64,16,128]{2,1,0:T(8,128)(2,1)S(1)}, u32[]{:S(2)}, u32[]{:S(2)}) %all-to-all-start) | async-done | bytes 262176 | tf_op jit(solution)/shard_map/all_to_all | solution.py:35
  28.5 1.9 %fusion.4 = bf16[1536,128]{1,0:T(8,128)(2,1)} fusion(bf16[1024,128]{1,0:T(8,128)(2,1)S(1)} %bitcast.85, s32[1024]{0:T(1024)S(1)} %add.214), kind=kOutput, calls=%fused_computation.8 | convolution fusion | flops 404422656 | bytes 659456 | tf_op jit(solution)/shard_map/mi,ic->mc/dot_general | solution.py:36
  30.4 5.4 %all-to-all-start.1 = ((bf16[64,24,128]{2,1,0:T(8,128)(2,1)}), bf16[64,24,128]{2,1,0:T(8,128)(2,1)S(1)}, u32[]{:S(2)}, u32[]{:S(2)}) async-start(bf16[64,24,128]{2,1,0:T(8,128)(2,1)} %bitcast.2), calls=%async_computation.1 | async-start | bytes 786432 | tf_op jit(solution)/shard_map/all_to_all | solution.py:38
  36.7 3.7 %reshape.494 = bf16[256,3200]{1,0:T(8,128)(2,1)S(1)} reshape(bf16[128,2,3200]{2,1,0:T(2,128)(2,1)} %param.8) | data formatting | bytes 3276800 | tf_op jit(solution)/shard_map/reshape | solution.py:188
  40.4 2.9 %fusion.83 = (bf16[256,3200]{1,0:T(8,128)(2,1)}, f32[256,3200]{1,0:T(8,128)}) fusion(bf16[256,3200]{1,0:T(8,128)(2,1)S(1)} %reshape.494, s32[256]{0:T(256)S(1)} %get-tuple-element.18), kind=kOutput, calls=%fused_computation.104 | convolution fusion | flops 420315136 | bytes 6554624 | tf_op jit(solution)/shard_map/wp,wc->pc/dot_general | solution.py:185
  43.3 7.5 %all-to-all-done.1 = bf16[64,24,128]{2,1,0:T(8,128)(2,1)S(1)} async-done(((bf16[64,24,128]{2,1,0:T(8,128)(2,1)}), bf16[64,24,128]{2,1,0:T(8,128)(2,1)S(1)}, u32[]{:S(2)}, u32[]{:S(2)}) %all-to-all-start.1) | async-done | bytes 393248 | tf_op jit(solution)/shard_map/all_to_all | solution.py:38
  51.3 8.4 %collective-permute-start.3 = (bf16[6,8,3200]{2,1,0:T(8,128)(2,1)S(1)}, bf16[6,8,3200]{2,1,0:T(8,128)(2,1)S(1)}, u32[]{:S(2)}, u32[]{:S(2)}) collective-permute-start(bf16[6,8,3200]{2,1,0:T(8,128)(2,1)S(1)} %reshape.489), channel_id=1, source_target_pairs={{0,4},{1,5},{2,6},{3,7},{4,0},{5,1},{6,2},{7,3},{8,12},{9,13},{10,... | collective-permute-start | bytes 921608 | tf_op jit(solution)/shard_map/ppermute | solution.py:49
  59.6 4.9 %collective-permute-start.2 = (bf16[6,8,3200]{2,1,0:T(8,128)(2,1)S(1)}, bf16[6,8,3200]{2,1,0:T(8,128)(2,1)S(1)}, u32[]{:S(2)}, u32[]{:S(2)}) collective-permute-start(bf16[6,8,3200]{2,1,0:T(8,128)(2,1)S(1)} %reshape.489), channel_id=1, source_target_pairs={{0,2},{1,3},{2,0},{3,1},{4,6},{5,7},{6,4},{7,5},{8,10},{9,11},{10,... | collective-permute-start | bytes 921608 | tf_op jit(solution)/shard_map/ppermute | solution.py:44
  64.6 3.0 %collective-permute-start.1 = (bf16[6,8,3200]{2,1,0:T(8,128)(2,1)S(1)}, bf16[6,8,3200]{2,1,0:T(8,128)(2,1)S(1)}, u32[]{:S(2)}, u32[]{:S(2)}) collective-permute-start(bf16[6,8,3200]{2,1,0:T(8,128)(2,1)S(1)} %reshape.489), channel_id=1, source_target_pairs={{0,3},{1,0},{2,1},{3,2},{4,7},{5,4},{6,5},{7,6},{8,11},{9,8},{10,9... | collective-permute-start | bytes 921608 | tf_op jit(solution)/shard_map/ppermute | solution.py:44
  67.6 2.8 %collective-permute-start = (bf16[6,8,3200]{2,1,0:T(8,128)(2,1)S(1)}, bf16[6,8,3200]{2,1,0:T(8,128)(2,1)S(1)}, u32[]{:S(2)}, u32[]{:S(2)}) collective-permute-start(bf16[6,8,3200]{2,1,0:T(8,128)(2,1)S(1)} %reshape.489), channel_id=1, source_target_pairs={{0,1},{1,2},{2,3},{3,0},{4,5},{5,6},{6,7},{7,4},{8,9},{9,10},{10,1... | collective-permute-start | bytes 921608 | tf_op jit(solution)/shard_map/ppermute | solution.py:44
  70.5 2.6 %collective-permute-start.6 = (bf16[6,8,3200]{2,1,0:T(8,128)(2,1)S(1)}, bf16[6,8,3200]{2,1,0:T(8,128)(2,1)S(1)}, u32[]{:S(2)}, u32[]{:S(2)}) collective-permute-start(bf16[6,8,3200]{2,1,0:T(8,128)(2,1)S(1)} %collective-permute-done.3), channel_id=1, source_target_pairs={{0,2},{1,3},{2,0},{3,1},{4,6},{5,7},{6,4},{7,5},{8,10},{9,11},{10,... | collective-permute-start | bytes 921608 | tf_op jit(solution)/shard_map/ppermute | solution.py:44
  73.0 4.5 %collective-permute-start.5 = (bf16[6,8,3200]{2,1,0:T(8,128)(2,1)S(1)}, bf16[6,8,3200]{2,1,0:T(8,128)(2,1)S(1)}, u32[]{:S(2)}, u32[]{:S(2)}) collective-permute-start(bf16[6,8,3200]{2,1,0:T(8,128)(2,1)S(1)} %collective-permute-done.3), channel_id=1, source_target_pairs={{0,3},{1,0},{2,1},{3,2},{4,7},{5,4},{6,5},{7,6},{8,11},{9,8},{10,9... | collective-permute-start | bytes 921608 | tf_op jit(solution)/shard_map/ppermute | solution.py:44
  77.6 8.0 %collective-permute-done = bf16[6,8,3200]{2,1,0:T(8,128)(2,1)S(1)} collective-permute-done((bf16[6,8,3200]{2,1,0:T(8,128)(2,1)S(1)}, bf16[6,8,3200]{2,1,0:T(8,128)(2,1)S(1)}, u32[]{:S(2)}, u32[]{:S(2)}) %collective-permute-start) | collective-permute-done | bytes 307232 | tf_op jit(solution)/shard_map/ppermute | solution.py:44
  85.5 1.9 %collective-permute-start.4 = (bf16[6,8,3200]{2,1,0:T(8,128)(2,1)S(1)}, bf16[6,8,3200]{2,1,0:T(8,128)(2,1)S(1)}, u32[]{:S(2)}, u32[]{:S(2)}) collective-permute-start(bf16[6,8,3200]{2,1,0:T(8,128)(2,1)S(1)} %collective-permute-done.3), channel_id=1, source_target_pairs={{0,1},{1,2},{2,3},{3,0},{4,5},{5,6},{6,7},{7,4},{8,9},{9,10},{10,1... | collective-permute-start | bytes 921608 | tf_op jit(solution)/shard_map/ppermute | solution.py:44
  87.6 7.9 %collective-permute-done.4 = bf16[6,8,3200]{2,1,0:T(8,128)(2,1)S(1)} collective-permute-done((bf16[6,8,3200]{2,1,0:T(8,128)(2,1)S(1)}, bf16[6,8,3200]{2,1,0:T(8,128)(2,1)S(1)}, u32[]{:S(2)}, u32[]{:S(2)}) %collective-permute-start.4) | collective-permute-done | bytes 307232 | tf_op jit(solution)/shard_map/ppermute | solution.py:44
  95.6 3.3 %weight_products.1 = (bf16[128,3200]{1,0:T(8,128)(2,1)}, bf16[128,3200]{1,0:T(8,128)(2,1)S(1)}, f32[1,3200]{1,0:T(1,128)S(1)}) custom-call(bf16[256,384]{1,0:T(8,128)(2,1)S(1)} %bitcast.78, bf16[384,3200]{1,0:T(8,128)(2,1)S(1)} %bitcast.76, bf16[256,3200]{1,0:T(8,128)(2,1)S(1)} %copy-done, f32[1,3200]{1,0:T(1,128)S(1)} %broadcast_in_dim.22.gain_ref), custom_call_target="tpu_custom_call" | custom-call | flops 629145600 | bytes 7340032 | tf_op jit(solution)/shard_map/weight_products/pallas_call | solution.py:95
  98.9 1.9 %collective-permute-start.7 = (bf16[128,3200]{1,0:T(8,128)(2,1)}, bf16[128,3200]{1,0:T(8,128)(2,1)}, u32[]{:S(2)}, u32[]{:S(2)}) collective-permute-start(bf16[128,3200]{1,0:T(8,128)(2,1)} %get-tuple-element.8), channel_id=1, source_target_pairs={{0,8},{8,0},{16,24},{24,16},{32,40},{40,32},{48,56},{56,48},{64,72... | collective-permute-start | bytes 2457608 | tf_op jit(solution)/shard_map/ppermute | solution.py:206
  101.0 13.8 %all_to_all.20.terms_ref = f32[16,1,3200]{2,1,0:T(1,128)S(1)} all-to-all(f32[16,1,3200]{2,1,0:T(1,128)S(1)} %broadcast_in_dim.23), channel_id=1, replica_groups={{0,1,2,3,4,5,6,7,8,9,10,11,12,13,14,15},{16,17,18,19,20,21,22,23,24,25,..., dimensions={0} | all-to-all | bytes 409600 | tf_op jit(solution)/shard_map/all_to_all | solution.py:76
  114.8 2.3 %outgoing_blocks.1 = bf16[32,4,4096]{2,1,0:T(4,128)(2,1)} custom-call(bf16[128,3200]{1,0:T(8,128)(2,1)S(1)} %get-tuple-element.7.kept_ref, bf16[128,3200]{1,0:T(8,128)(2,1)} %collective-permute-done.7.taken_ref, f32[16,1,3200]{2,1,0:T(1,128)S(1)} %all_to_all.20.terms_ref), custom_call_target="tpu_custom_call" | custom-call | flops 409600 | bytes 4194304 | tf_op jit(solution)/shard_map/outgoing_blocks/pallas_call | solution.py:142
  117.1 10.0 %all-to-all-start.3 = ((bf16[32,4,4096]{2,1,0:T(4,128)(2,1)}), bf16[32,4,4096]{2,1,0:T(4,128)(2,1)S(1)}, u32[]{:S(2)}, u32[]{:S(2)}) async-start(bf16[32,4,4096]{2,1,0:T(4,128)(2,1)} %outgoing_blocks.1), calls=%async_computation.3 | async-start | bytes 2097152 | tf_op jit(solution)/shard_map/all_to_all | solution.py:212
  127.1 3.6 %convolution_convert_fusion.3 = bf16[384,256]{1,0:T(8,128)(2,1)} fusion(bf16[384,3200]{1,0:T(8,128)(2,1)S(1)} %bitcast.77, f32[256,3200]{1,0:T(8,128)} %get-tuple-element.17, f32[3200]{0:T(1024)S(1)} %copy-done.7, s32[256]{0:T(256)S(1)} %get-tuple-element.19), kind=kOutput, calls=%fused_computation.23 | convolution fusion | flops 681377792 | bytes 5944832 | tf_op jit(solution)/shard_map/np,wp->nw/dot_general | solution.py:221
  130.7 1.5 gather_fusion.1
  138.7 17.3 %all-to-all-done.3 = bf16[32,4,4096]{2,1,0:T(4,128)(2,1)S(1)} async-done(((bf16[32,4,4096]{2,1,0:T(4,128)(2,1)}), bf16[32,4,4096]{2,1,0:T(4,128)(2,1)S(1)}, u32[]{:S(2)}, u32[]{:S(2)}) %all-to-all-start.3) | async-done | bytes 1048608 | tf_op jit(solution)/shard_map/all_to_all | solution.py:212
  (83 shorter events, 16.1 us)
Async XLA Ops:
  0.6 17.6 %copy-start.2 = (bf16[3,6,64,256]{3,2,1,0:T(8,128)(2,1)S(1)}, bf16[3,6,64,256]{3,2,1,0:T(8,128)(2,1)}, u32[]{:S(2)}) copy-start(bf16[3,6,64,256]{3,2,1,0:T(8,128)(2,1)} %param.6) | copy-start | bytes 1769476
  2.6 25.9 %all-to-all-start = ((bf16[64,16,128]{2,1,0:T(8,128)(2,1)}), bf16[64,16,128]{2,1,0:T(8,128)(2,1)S(1)}, u32[]{:S(2)}, u32[]{:S(2)}) async-start(bf16[64,16,128]{2,1,0:T(8,128)(2,1)} %pad.9.clone), calls=%async_computation | async-start | bytes 524288 | tf_op jit(solution)/shard_map/all_to_all | solution.py:35
  18.4 2.3 %copy-start.3 = (bf16[6,64,2,128]{3,2,1,0:T(2,128)(2,1)}, bf16[6,64,2,128]{3,2,1,0:T(2,128)(2,1)S(1)}, u32[]{:S(2)}) copy-start(bf16[6,64,2,128]{3,2,1,0:T(2,128)(2,1)S(1)} %squeeze.12) | copy-start | bytes 589828
  18.5 11.9 %copy-start.5 = (bf16[6,64,2,128]{3,2,1,0:T(2,128)(2,1)}, bf16[6,64,2,128]{3,2,1,0:T(2,128)(2,1)S(1)}, u32[]{:S(2)}) copy-start(bf16[6,64,2,128]{3,2,1,0:T(2,128)(2,1)S(1)} %squeeze.13) | copy-start | bytes 589828
  18.5 11.9 %copy-start.1 = (bf16[6,64,2,128]{3,2,1,0:T(2,128)(2,1)}, bf16[6,64,2,128]{3,2,1,0:T(2,128)(2,1)S(1)}, u32[]{:S(2)}) copy-start(bf16[6,64,2,128]{3,2,1,0:T(2,128)(2,1)S(1)} %squeeze.14) | copy-start | bytes 589828
  28.5 7.4 %copy-start.7 = (f32[3200]{0:T(1024)S(1)}, f32[3200]{0:T(1024)}, u32[]{:S(2)}) copy-start(f32[3200]{0:T(1024)} %param.9) | copy-start | bytes 38404
  30.4 20.4 %all-to-all-start.1 = ((bf16[64,24,128]{2,1,0:T(8,128)(2,1)}), bf16[64,24,128]{2,1,0:T(8,128)(2,1)S(1)}, u32[]{:S(2)}, u32[]{:S(2)}) async-start(bf16[64,24,128]{2,1,0:T(8,128)(2,1)} %bitcast.2), calls=%async_computation.1 | async-start | bytes 786432 | tf_op jit(solution)/shard_map/all_to_all | solution.py:38
  51.3 44.3 %copy-start = (bf16[256,3200]{1,0:T(8,128)(2,1)S(1)}, bf16[256,3200]{1,0:T(8,128)(2,1)}, u32[]{:S(2)}) copy-start(bf16[256,3200]{1,0:T(8,128)(2,1)} %get-tuple-element.16.weight_ref) | copy-start | bytes 4915204
  51.3 19.2 %collective-permute-start.3 = (bf16[6,8,3200]{2,1,0:T(8,128)(2,1)S(1)}, bf16[6,8,3200]{2,1,0:T(8,128)(2,1)S(1)}, u32[]{:S(2)}, u32[]{:S(2)}) collective-permute-start(bf16[6,8,3200]{2,1,0:T(8,128)(2,1)S(1)} %reshape.489), channel_id=1, source_target_pairs={{0,4},{1,5},{2,6},{3,7},{4,0},{5,1},{6,2},{7,3},{8,12},{9,13},{10,... | collective-permute-start | bytes 921608 | tf_op jit(solution)/shard_map/ppermute | solution.py:49
  59.6 27.9 %collective-permute-start.2 = (bf16[6,8,3200]{2,1,0:T(8,128)(2,1)S(1)}, bf16[6,8,3200]{2,1,0:T(8,128)(2,1)S(1)}, u32[]{:S(2)}, u32[]{:S(2)}) collective-permute-start(bf16[6,8,3200]{2,1,0:T(8,128)(2,1)S(1)} %reshape.489), channel_id=1, source_target_pairs={{0,2},{1,3},{2,0},{3,1},{4,6},{5,7},{6,4},{7,5},{8,10},{9,11},{10,... | collective-permute-start | bytes 921608 | tf_op jit(solution)/shard_map/ppermute | solution.py:44
  64.6 22.9 %collective-permute-start.1 = (bf16[6,8,3200]{2,1,0:T(8,128)(2,1)S(1)}, bf16[6,8,3200]{2,1,0:T(8,128)(2,1)S(1)}, u32[]{:S(2)}, u32[]{:S(2)}) collective-permute-start(bf16[6,8,3200]{2,1,0:T(8,128)(2,1)S(1)} %reshape.489), channel_id=1, source_target_pairs={{0,3},{1,0},{2,1},{3,2},{4,7},{5,4},{6,5},{7,6},{8,11},{9,8},{10,9... | collective-permute-start | bytes 921608 | tf_op jit(solution)/shard_map/ppermute | solution.py:44
  67.6 17.9 %collective-permute-start = (bf16[6,8,3200]{2,1,0:T(8,128)(2,1)S(1)}, bf16[6,8,3200]{2,1,0:T(8,128)(2,1)S(1)}, u32[]{:S(2)}, u32[]{:S(2)}) collective-permute-start(bf16[6,8,3200]{2,1,0:T(8,128)(2,1)S(1)} %reshape.489), channel_id=1, source_target_pairs={{0,1},{1,2},{2,3},{3,0},{4,5},{5,6},{6,7},{7,4},{8,9},{9,10},{10,1... | collective-permute-start | bytes 921608 | tf_op jit(solution)/shard_map/ppermute | solution.py:44
  70.5 25.1 %collective-permute-start.6 = (bf16[6,8,3200]{2,1,0:T(8,128)(2,1)S(1)}, bf16[6,8,3200]{2,1,0:T(8,128)(2,1)S(1)}, u32[]{:S(2)}, u32[]{:S(2)}) collective-permute-start(bf16[6,8,3200]{2,1,0:T(8,128)(2,1)S(1)} %collective-permute-done.3), channel_id=1, source_target_pairs={{0,2},{1,3},{2,0},{3,1},{4,6},{5,7},{6,4},{7,5},{8,10},{9,11},{10,... | collective-permute-start | bytes 921608 | tf_op jit(solution)/shard_map/ppermute | solution.py:44
  73.0 22.5 %collective-permute-start.5 = (bf16[6,8,3200]{2,1,0:T(8,128)(2,1)S(1)}, bf16[6,8,3200]{2,1,0:T(8,128)(2,1)S(1)}, u32[]{:S(2)}, u32[]{:S(2)}) collective-permute-start(bf16[6,8,3200]{2,1,0:T(8,128)(2,1)S(1)} %collective-permute-done.3), channel_id=1, source_target_pairs={{0,3},{1,0},{2,1},{3,2},{4,7},{5,4},{6,5},{7,6},{8,11},{9,8},{10,9... | collective-permute-start | bytes 921608 | tf_op jit(solution)/shard_map/ppermute | solution.py:44
  85.5 9.9 %collective-permute-start.4 = (bf16[6,8,3200]{2,1,0:T(8,128)(2,1)S(1)}, bf16[6,8,3200]{2,1,0:T(8,128)(2,1)S(1)}, u32[]{:S(2)}, u32[]{:S(2)}) collective-permute-start(bf16[6,8,3200]{2,1,0:T(8,128)(2,1)S(1)} %collective-permute-done.3), channel_id=1, source_target_pairs={{0,1},{1,2},{2,3},{3,0},{4,5},{5,6},{6,7},{7,4},{8,9},{9,10},{10,1... | collective-permute-start | bytes 921608 | tf_op jit(solution)/shard_map/ppermute | solution.py:44
  98.9 15.8 %collective-permute-start.7 = (bf16[128,3200]{1,0:T(8,128)(2,1)}, bf16[128,3200]{1,0:T(8,128)(2,1)}, u32[]{:S(2)}, u32[]{:S(2)}) collective-permute-start(bf16[128,3200]{1,0:T(8,128)(2,1)} %get-tuple-element.8), channel_id=1, source_target_pairs={{0,8},{8,0},{16,24},{24,16},{32,40},{40,32},{48,56},{56,48},{64,72... | collective-permute-start | bytes 2457608 | tf_op jit(solution)/shard_map/ppermute | solution.py:206
  117.1 39.0 %all-to-all-start.3 = ((bf16[32,4,4096]{2,1,0:T(4,128)(2,1)}), bf16[32,4,4096]{2,1,0:T(4,128)(2,1)S(1)}, u32[]{:S(2)}, u32[]{:S(2)}) async-start(bf16[32,4,4096]{2,1,0:T(4,128)(2,1)} %outgoing_blocks.1), calls=%async_computation.3 | async-start | bytes 2097152 | tf_op jit(solution)/shard_map/all_to_all | solution.py:212
  130.7 4.6 %copy-start.6 = (bf16[6,64,2,128]{3,2,1,0:T(2,128)(2,1)S(1)}, bf16[6,64,2,128]{3,2,1,0:T(2,128)(2,1)}, u32[]{:S(2)}) copy-start(bf16[6,64,2,128]{3,2,1,0:T(2,128)(2,1)} %copy-done.5) | copy-start | bytes 589828
  134.9 2.2 %copy-start.4 = (bf16[6,64,2,128]{3,2,1,0:T(2,128)(2,1)S(1)}, bf16[6,64,2,128]{3,2,1,0:T(2,128)(2,1)}, u32[]{:S(2)}) copy-start(bf16[6,64,2,128]{3,2,1,0:T(2,128)(2,1)} %copy-done.3) | copy-start | bytes 589828

commit v6 on v5

--- a/solution.py
+++ b/solution.py
@@ -14,6 +14,33 @@
         high, x = index // N_X, index % N_X
         pairs.append((index, (high + shift_hi) % 2 * N_X + (x + shift_x) % N_X))
     return pairs
+
+
+def spread_body(image_ref, out_ref):
+    images, tokens, width = image_ref.shape
+    part, lanes = 4, 128
+    empty = jnp.zeros((part, lanes), jnp.float32)
+    for run in range(width // lanes):
+        tiles = [
+            image_ref[image, :, run * lanes : (run + 1) * lanes].astype(jnp.float32)
+            for image in range(images)
+        ]
+        for index in range(tokens // part):
+            rows = [tile[index * part : (index + 1) * part] for tile in tiles] + [empty]
+            piece = run * (tokens // part) + index
+            out_ref[piece] = jnp.concatenate(rows).astype(jnp.bfloat16)
+    used = width // lanes * (tokens // part)
+    out_ref[used:] = jnp.zeros((out_ref.shape[0] - used,) + out_ref.shape[1:], jnp.bfloat16)
+
+
+def spread_pieces(grad_out, replicas):
+    rows = 4 * (grad_out.shape[0] + 1)
+    return pl.pallas_call(
+        spread_body,
+        out_shape=jax.ShapeDtypeStruct((replicas, rows, 128), grad_out.dtype),
+        cost_estimate=pl.CostEstimate(flops=0, bytes_accessed=2**19, transcendentals=0),
+        name="spread_pieces",
+    )(grad_out)
 
 
 def deal(owner, grad_out, slot_count):
@@ -29,9 +56,7 @@
     rows = jnp.arange(replicas * slot_count * part, dtype=jnp.int32)
     chosen = (rows[:, None] == row_of[None, :]).astype(grad_out.dtype)
 
-    spread = grad_out.reshape(images, parts, part, runs, lanes).transpose(3, 1, 0, 2, 4)
-    spread = spread.reshape(pieces, images * part, lanes)
-    spread = jnp.pad(spread, ((0, replicas - pieces), (0, part), (0, 0)))
+    spread = spread_pieces(grad_out, replicas)
     held = lax.all_to_all(spread, "replica", 0, 0).reshape(replicas * (images + 1) * part, lanes)
     dealt = jnp.einsum("mi,ic->mc", chosen, held, preferred_element_type=jnp.float32)
     dealt = dealt.astype(grad_out.dtype).reshape(replicas, slot_count * part, lanes)

time: 159 us -> 158 us (level)
  Pallas kernels: 5.65 us -> 7.32 us
    pallas_call x0 -> x1, Pallas kernels: none -> 1.66 us  [spread_pieces(): pl.pallas_call(spread_body, out_shape=jax.ShapeDtypeStruct((replicas, row...]
  transfers between devices with their start and end apart: 11 -> 11, of which waited for: 5 -> 5; matrix products, arithmetic and copies ran while one was open for 15% -> 16% of each run, Pallas kernels for 0% -> 0%
where the time goes in v6:
time: 158 us
  starting transfers between devices  58.9 us (37%)
  waiting for transfers between devices  47.4 us (30%)
  matrix products  14.6 us (9%)
  blocking collectives  13.8 us (9%)
  local copies, waits for them, and re-layouts  11.1 us (7%)
  Pallas kernels  7.32 us (5%)
  other arithmetic  3.25 us (2%)
    ppermute x6, starting transfers between devices, ring_gather(): lax.ppermute(block, 'tensor', tensor_step(0, k))  19.8 us
    all_to_all x1, waiting for transfers between devices, local(): lax.all_to_all(outgoing, 'replica', 0, 0, axis_index_groups=columns)  17.3 us
    ppermute x6, waiting for transfers between devices, ring_gather(): lax.ppermute(block, 'tensor', tensor_step(0, k))  15.8 us
    all_to_all x1, blocking collectives, over_chip_and_tensor(): lax.all_to_all(copies, ('replica', 'tensor'), 0, 0, axis_index_groups=near)  13.8 us
    all_to_all x1, starting transfers between devices, deal(): lax.all_to_all(spread, 'replica', 0, 0)  13.5 us
    all_to_all x1, starting transfers between devices, local(): lax.all_to_all(outgoing, 'replica', 0, 0, axis_index_groups=columns)  9.97 us
    ppermute x1, starting transfers between devices, gather_tokens(): other = lax.ppermute(block, 'tensor', tensor_step(1, 0))  8.35 us
    all_to_all x1, waiting for transfers between devices, deal(): mine = lax.all_to_all(dealt, 'replica', 0, 0)[:pieces]  7.52 us
  transfers between devices with their start and end apart: 11, of which 5 were waited for; matrix products, arithmetic and copies ran while one was open for 16% of the time, Pallas kernels for 0%

profile of v6, /device:TPU:8, one launch (start us, length us, event | category | flops | bytes accessed | tf_op | source)
XLA Modules:
  0.0 157.5 jit_solution(7876947267403157984)
XLA Ops:
  0.6 1.7 %spread_pieces.1 = bf16[64,16,128]{2,1,0:T(8,128)(2,1)} custom-call(bf16[3,8,3200]{2,1,0:T(8,128)(2,1)} %image_ref.1), custom_call_target="tpu_custom_call" | custom-call | bytes 524288 | tf_op jit(solution)/shard_map/spread_pieces/pallas_call | solution.py:38
  2.3 13.5 %all-to-all-start = ((bf16[64,16,128]{2,1,0:T(8,128)(2,1)}), bf16[64,16,128]{2,1,0:T(8,128)(2,1)S(1)}, u32[]{:S(2)}, u32[]{:S(2)}) async-start(bf16[64,16,128]{2,1,0:T(8,128)(2,1)} %spread_pieces.1), calls=%async_computation | async-start | bytes 524288 | tf_op jit(solution)/shard_map/all_to_all | solution.py:60
  21.5 6.7 %all-to-all-done = bf16[64,16,128]{2,1,0:T(8,128)(2,1)S(1)} async-done(((bf16[64,16,128]{2,1,0:T(8,128)(2,1)}), bf16[64,16,128]{2,1,0:T(8,128)(2,1)S(1)}, u32[]{:S(2)}, u32[]{:S(2)}) %all-to-all-start) | async-done | bytes 262176 | tf_op jit(solution)/shard_map/all_to_all | solution.py:60
  28.2 1.9 %fusion.4 = bf16[1536,128]{1,0:T(8,128)(2,1)} fusion(bf16[1024,128]{1,0:T(8,128)(2,1)S(1)} %bitcast.83, s32[1024]{0:T(1024)S(1)} %add.212), kind=kOutput, calls=%fused_computation.8 | convolution fusion | flops 404422656 | bytes 659456 | tf_op jit(solution)/shard_map/mi,ic->mc/dot_general | solution.py:61
  30.1 5.4 %all-to-all-start.1 = ((bf16[64,24,128]{2,1,0:T(8,128)(2,1)}), bf16[64,24,128]{2,1,0:T(8,128)(2,1)S(1)}, u32[]{:S(2)}, u32[]{:S(2)}) async-start(bf16[64,24,128]{2,1,0:T(8,128)(2,1)} %bitcast.1), calls=%async_computation.1 | async-start | bytes 786432 | tf_op jit(solution)/shard_map/all_to_all | solution.py:63
  36.4 3.7 %reshape.486 = bf16[256,3200]{1,0:T(8,128)(2,1)S(1)} reshape(bf16[128,2,3200]{2,1,0:T(2,128)(2,1)} %param.8) | data formatting | bytes 3276800 | tf_op jit(solution)/shard_map/reshape | solution.py:213
  40.1 2.9 %fusion.83 = (bf16[256,3200]{1,0:T(8,128)(2,1)}, f32[256,3200]{1,0:T(8,128)}) fusion(bf16[256,3200]{1,0:T(8,128)(2,1)S(1)} %reshape.486, s32[256]{0:T(256)S(1)} %get-tuple-element.18), kind=kOutput, calls=%fused_computation.104 | convolution fusion | flops 420315136 | bytes 6554624 | tf_op jit(solution)/shard_map/wp,wc->pc/dot_general | solution.py:210
  43.0 7.5 %all-to-all-done.1 = bf16[64,24,128]{2,1,0:T(8,128)(2,1)S(1)} async-done(((bf16[64,24,128]{2,1,0:T(8,128)(2,1)}), bf16[64,24,128]{2,1,0:T(8,128)(2,1)S(1)}, u32[]{:S(2)}, u32[]{:S(2)}) %all-to-all-start.1) | async-done | bytes 393248 | tf_op jit(solution)/shard_map/all_to_all | solution.py:63
  51.0 8.4 %collective-permute-start.3 = (bf16[6,8,3200]{2,1,0:T(8,128)(2,1)S(1)}, bf16[6,8,3200]{2,1,0:T(8,128)(2,1)S(1)}, u32[]{:S(2)}, u32[]{:S(2)}) collective-permute-start(bf16[6,8,3200]{2,1,0:T(8,128)(2,1)S(1)} %reshape.481), channel_id=1, source_target_pairs={{0,4},{1,5},{2,6},{3,7},{4,0},{5,1},{6,2},{7,3},{8,12},{9,13},{10,... | collective-permute-start | bytes 921608 | tf_op jit(solution)/shard_map/ppermute | solution.py:74
  59.3 4.9 %collective-permute-start.2 = (bf16[6,8,3200]{2,1,0:T(8,128)(2,1)S(1)}, bf16[6,8,3200]{2,1,0:T(8,128)(2,1)S(1)}, u32[]{:S(2)}, u32[]{:S(2)}) collective-permute-start(bf16[6,8,3200]{2,1,0:T(8,128)(2,1)S(1)} %reshape.481), channel_id=1, source_target_pairs={{0,2},{1,3},{2,0},{3,1},{4,6},{5,7},{6,4},{7,5},{8,10},{9,11},{10,... | collective-permute-start | bytes 921608 | tf_op jit(solution)/shard_map/ppermute | solution.py:69
  64.3 3.0 %collective-permute-start.1 = (bf16[6,8,3200]{2,1,0:T(8,128)(2,1)S(1)}, bf16[6,8,3200]{2,1,0:T(8,128)(2,1)S(1)}, u32[]{:S(2)}, u32[]{:S(2)}) collective-permute-start(bf16[6,8,3200]{2,1,0:T(8,128)(2,1)S(1)} %reshape.481), channel_id=1, source_target_pairs={{0,3},{1,0},{2,1},{3,2},{4,7},{5,4},{6,5},{7,6},{8,11},{9,8},{10,9... | collective-permute-start | bytes 921608 | tf_op jit(solution)/shard_map/ppermute | solution.py:69
  67.3 2.8 %collective-permute-start = (bf16[6,8,3200]{2,1,0:T(8,128)(2,1)S(1)}, bf16[6,8,3200]{2,1,0:T(8,128)(2,1)S(1)}, u32[]{:S(2)}, u32[]{:S(2)}) collective-permute-start(bf16[6,8,3200]{2,1,0:T(8,128)(2,1)S(1)} %reshape.481), channel_id=1, source_target_pairs={{0,1},{1,2},{2,3},{3,0},{4,5},{5,6},{6,7},{7,4},{8,9},{9,10},{10,1... | collective-permute-start | bytes 921608 | tf_op jit(solution)/shard_map/ppermute | solution.py:69
  70.2 2.6 %collective-permute-start.6 = (bf16[6,8,3200]{2,1,0:T(8,128)(2,1)S(1)}, bf16[6,8,3200]{2,1,0:T(8,128)(2,1)S(1)}, u32[]{:S(2)}, u32[]{:S(2)}) collective-permute-start(bf16[6,8,3200]{2,1,0:T(8,128)(2,1)S(1)} %collective-permute-done.3), channel_id=1, source_target_pairs={{0,2},{1,3},{2,0},{3,1},{4,6},{5,7},{6,4},{7,5},{8,10},{9,11},{10,... | collective-permute-start | bytes 921608 | tf_op jit(solution)/shard_map/ppermute | solution.py:69
  72.7 4.5 %collective-permute-start.5 = (bf16[6,8,3200]{2,1,0:T(8,128)(2,1)S(1)}, bf16[6,8,3200]{2,1,0:T(8,128)(2,1)S(1)}, u32[]{:S(2)}, u32[]{:S(2)}) collective-permute-start(bf16[6,8,3200]{2,1,0:T(8,128)(2,1)S(1)} %collective-permute-done.3), channel_id=1, source_target_pairs={{0,3},{1,0},{2,1},{3,2},{4,7},{5,4},{6,5},{7,6},{8,11},{9,8},{10,9... | collective-permute-start | bytes 921608 | tf_op jit(solution)/shard_map/ppermute | solution.py:69
  77.3 8.0 %collective-permute-done = bf16[6,8,3200]{2,1,0:T(8,128)(2,1)S(1)} collective-permute-done((bf16[6,8,3200]{2,1,0:T(8,128)(2,1)S(1)}, bf16[6,8,3200]{2,1,0:T(8,128)(2,1)S(1)}, u32[]{:S(2)}, u32[]{:S(2)}) %collective-permute-start) | collective-permute-done | bytes 307232 | tf_op jit(solution)/shard_map/ppermute | solution.py:69
  85.2 1.9 %collective-permute-start.4 = (bf16[6,8,3200]{2,1,0:T(8,128)(2,1)S(1)}, bf16[6,8,3200]{2,1,0:T(8,128)(2,1)S(1)}, u32[]{:S(2)}, u32[]{:S(2)}) collective-permute-start(bf16[6,8,3200]{2,1,0:T(8,128)(2,1)S(1)} %collective-permute-done.3), channel_id=1, source_target_pairs={{0,1},{1,2},{2,3},{3,0},{4,5},{5,6},{6,7},{7,4},{8,9},{9,10},{10,1... | collective-permute-start | bytes 921608 | tf_op jit(solution)/shard_map/ppermute | solution.py:69
  87.3 7.9 %collective-permute-done.4 = bf16[6,8,3200]{2,1,0:T(8,128)(2,1)S(1)} collective-permute-done((bf16[6,8,3200]{2,1,0:T(8,128)(2,1)S(1)}, bf16[6,8,3200]{2,1,0:T(8,128)(2,1)S(1)}, u32[]{:S(2)}, u32[]{:S(2)}) %collective-permute-start.4) | collective-permute-done | bytes 307232 | tf_op jit(solution)/shard_map/ppermute | solution.py:69
  95.3 3.4 %weight_products.1 = (bf16[128,3200]{1,0:T(8,128)(2,1)}, bf16[128,3200]{1,0:T(8,128)(2,1)S(1)}, f32[1,3200]{1,0:T(1,128)S(1)}) custom-call(bf16[256,384]{1,0:T(8,128)(2,1)S(1)} %bitcast.77, bf16[384,3200]{1,0:T(8,128)(2,1)S(1)} %bitcast.75, bf16[256,3200]{1,0:T(8,128)(2,1)S(1)} %copy-done, f32[1,3200]{1,0:T(1,128)S(1)} %broadcast_in_dim.22.gain_ref), custom_call_target="tpu_custom_call" | custom-call | flops 629145600 | bytes 7340032 | tf_op jit(solution)/shard_map/weight_products/pallas_call | solution.py:120
  98.7 1.9 %collective-permute-start.7 = (bf16[128,3200]{1,0:T(8,128)(2,1)}, bf16[128,3200]{1,0:T(8,128)(2,1)}, u32[]{:S(2)}, u32[]{:S(2)}) collective-permute-start(bf16[128,3200]{1,0:T(8,128)(2,1)} %get-tuple-element.8), channel_id=1, source_target_pairs={{0,8},{8,0},{16,24},{24,16},{32,40},{40,32},{48,56},{56,48},{64,72... | collective-permute-start | bytes 2457608 | tf_op jit(solution)/shard_map/ppermute | solution.py:231
  100.7 13.8 %all_to_all.20.terms_ref = f32[16,1,3200]{2,1,0:T(1,128)S(1)} all-to-all(f32[16,1,3200]{2,1,0:T(1,128)S(1)} %broadcast_in_dim.23), channel_id=1, replica_groups={{0,1,2,3,4,5,6,7,8,9,10,11,12,13,14,15},{16,17,18,19,20,21,22,23,24,25,..., dimensions={0} | all-to-all | bytes 409600 | tf_op jit(solution)/shard_map/all_to_all | solution.py:101
  114.5 2.3 %outgoing_blocks.1 = bf16[32,4,4096]{2,1,0:T(4,128)(2,1)} custom-call(bf16[128,3200]{1,0:T(8,128)(2,1)S(1)} %get-tuple-element.7.kept_ref, bf16[128,3200]{1,0:T(8,128)(2,1)} %collective-permute-done.7.taken_ref, f32[16,1,3200]{2,1,0:T(1,128)S(1)} %all_to_all.20.terms_ref), custom_call_target="tpu_custom_call" | custom-call | flops 409600 | bytes 4194304 | tf_op jit(solution)/shard_map/outgoing_blocks/pallas_call | solution.py:167
  116.8 10.0 %all-to-all-start.3 = ((bf16[32,4,4096]{2,1,0:T(4,128)(2,1)}), bf16[32,4,4096]{2,1,0:T(4,128)(2,1)S(1)}, u32[]{:S(2)}, u32[]{:S(2)}) async-start(bf16[32,4,4096]{2,1,0:T(4,128)(2,1)} %outgoing_blocks.1), calls=%async_computation.3 | async-start | bytes 2097152 | tf_op jit(solution)/shard_map/all_to_all | solution.py:237
  126.8 3.6 %convolution_convert_fusion.3 = bf16[384,256]{1,0:T(8,128)(2,1)} fusion(bf16[384,3200]{1,0:T(8,128)(2,1)S(1)} %bitcast.76, f32[256,3200]{1,0:T(8,128)} %get-tuple-element.17, f32[3200]{0:T(1024)S(1)} %copy-done.6, s32[256]{0:T(256)S(1)} %get-tuple-element.19), kind=kOutput, calls=%fused_computation.23 | convolution fusion | flops 681377792 | bytes 5944832 | tf_op jit(solution)/shard_map/np,wp->nw/dot_general | solution.py:246
  138.5 17.3 %all-to-all-done.3 = bf16[32,4,4096]{2,1,0:T(4,128)(2,1)S(1)} async-done(((bf16[32,4,4096]{2,1,0:T(4,128)(2,1)}), bf16[32,4,4096]{2,1,0:T(4,128)(2,1)S(1)}, u32[]{:S(2)}, u32[]{:S(2)}) %all-to-all-start.3) | async-done | bytes 1048608 | tf_op jit(solution)/shard_map/all_to_all | solution.py:237
  (78 shorter events, 16.8 us)
Async XLA Ops:
  2.3 25.9 %all-to-all-start = ((bf16[64,16,128]{2,1,0:T(8,128)(2,1)}), bf16[64,16,128]{2,1,0:T(8,128)(2,1)S(1)}, u32[]{:S(2)}, u32[]{:S(2)}) async-start(bf16[64,16,128]{2,1,0:T(8,128)(2,1)} %spread_pieces.1), calls=%async_computation | async-start | bytes 524288 | tf_op jit(solution)/shard_map/all_to_all | solution.py:60
  19.2 2.3 %copy-start.2 = (bf16[6,64,2,128]{3,2,1,0:T(2,128)(2,1)}, bf16[6,64,2,128]{3,2,1,0:T(2,128)(2,1)S(1)}, u32[]{:S(2)}) copy-start(bf16[6,64,2,128]{3,2,1,0:T(2,128)(2,1)S(1)} %squeeze.12) | copy-start | bytes 589828
  19.3 10.8 %copy-start.4 = (bf16[6,64,2,128]{3,2,1,0:T(2,128)(2,1)}, bf16[6,64,2,128]{3,2,1,0:T(2,128)(2,1)S(1)}, u32[]{:S(2)}) copy-start(bf16[6,64,2,128]{3,2,1,0:T(2,128)(2,1)S(1)} %squeeze.13) | copy-start | bytes 589828
  19.3 10.8 %copy-start.1 = (bf16[6,64,2,128]{3,2,1,0:T(2,128)(2,1)}, bf16[6,64,2,128]{3,2,1,0:T(2,128)(2,1)S(1)}, u32[]{:S(2)}) copy-start(bf16[6,64,2,128]{3,2,1,0:T(2,128)(2,1)S(1)} %squeeze.14) | copy-start | bytes 589828
  28.2 7.4 %copy-start.6 = (f32[3200]{0:T(1024)S(1)}, f32[3200]{0:T(1024)}, u32[]{:S(2)}) copy-start(f32[3200]{0:T(1024)} %param.9) | copy-start | bytes 38404
  30.1 20.4 %all-to-all-start.1 = ((bf16[64,24,128]{2,1,0:T(8,128)(2,1)}), bf16[64,24,128]{2,1,0:T(8,128)(2,1)S(1)}, u32[]{:S(2)}, u32[]{:S(2)}) async-start(bf16[64,24,128]{2,1,0:T(8,128)(2,1)} %bitcast.1), calls=%async_computation.1 | async-start | bytes 786432 | tf_op jit(solution)/shard_map/all_to_all | solution.py:63
  51.0 44.3 %copy-start = (bf16[256,3200]{1,0:T(8,128)(2,1)S(1)}, bf16[256,3200]{1,0:T(8,128)(2,1)}, u32[]{:S(2)}) copy-start(bf16[256,3200]{1,0:T(8,128)(2,1)} %get-tuple-element.16.weight_ref) | copy-start | bytes 4915204
  51.0 19.2 %collective-permute-start.3 = (bf16[6,8,3200]{2,1,0:T(8,128)(2,1)S(1)}, bf16[6,8,3200]{2,1,0:T(8,128)(2,1)S(1)}, u32[]{:S(2)}, u32[]{:S(2)}) collective-permute-start(bf16[6,8,3200]{2,1,0:T(8,128)(2,1)S(1)} %reshape.481), channel_id=1, source_target_pairs={{0,4},{1,5},{2,6},{3,7},{4,0},{5,1},{6,2},{7,3},{8,12},{9,13},{10,... | collective-permute-start | bytes 921608 | tf_op jit(solution)/shard_map/ppermute | solution.py:74
  59.3 27.9 %collective-permute-start.2 = (bf16[6,8,3200]{2,1,0:T(8,128)(2,1)S(1)}, bf16[6,8,3200]{2,1,0:T(8,128)(2,1)S(1)}, u32[]{:S(2)}, u32[]{:S(2)}) collective-permute-start(bf16[6,8,3200]{2,1,0:T(8,128)(2,1)S(1)} %reshape.481), channel_id=1, source_target_pairs={{0,2},{1,3},{2,0},{3,1},{4,6},{5,7},{6,4},{7,5},{8,10},{9,11},{10,... | collective-permute-start | bytes 921608 | tf_op jit(solution)/shard_map/ppermute | solution.py:69
  64.3 22.9 %collective-permute-start.1 = (bf16[6,8,3200]{2,1,0:T(8,128)(2,1)S(1)}, bf16[6,8,3200]{2,1,0:T(8,128)(2,1)S(1)}, u32[]{:S(2)}, u32[]{:S(2)}) collective-permute-start(bf16[6,8,3200]{2,1,0:T(8,128)(2,1)S(1)} %reshape.481), channel_id=1, source_target_pairs={{0,3},{1,0},{2,1},{3,2},{4,7},{5,4},{6,5},{7,6},{8,11},{9,8},{10,9... | collective-permute-start | bytes 921608 | tf_op jit(solution)/shard_map/ppermute | solution.py:69
  67.3 17.9 %collective-permute-start = (bf16[6,8,3200]{2,1,0:T(8,128)(2,1)S(1)}, bf16[6,8,3200]{2,1,0:T(8,128)(2,1)S(1)}, u32[]{:S(2)}, u32[]{:S(2)}) collective-permute-start(bf16[6,8,3200]{2,1,0:T(8,128)(2,1)S(1)} %reshape.481), channel_id=1, source_target_pairs={{0,1},{1,2},{2,3},{3,0},{4,5},{5,6},{6,7},{7,4},{8,9},{9,10},{10,1... | collective-permute-start | bytes 921608 | tf_op jit(solution)/shard_map/ppermute | solution.py:69
  70.2 25.1 %collective-permute-start.6 = (bf16[6,8,3200]{2,1,0:T(8,128)(2,1)S(1)}, bf16[6,8,3200]{2,1,0:T(8,128)(2,1)S(1)}, u32[]{:S(2)}, u32[]{:S(2)}) collective-permute-start(bf16[6,8,3200]{2,1,0:T(8,128)(2,1)S(1)} %collective-permute-done.3), channel_id=1, source_target_pairs={{0,2},{1,3},{2,0},{3,1},{4,6},{5,7},{6,4},{7,5},{8,10},{9,11},{10,... | collective-permute-start | bytes 921608 | tf_op jit(solution)/shard_map/ppermute | solution.py:69
  72.7 22.5 %collective-permute-start.5 = (bf16[6,8,3200]{2,1,0:T(8,128)(2,1)S(1)}, bf16[6,8,3200]{2,1,0:T(8,128)(2,1)S(1)}, u32[]{:S(2)}, u32[]{:S(2)}) collective-permute-start(bf16[6,8,3200]{2,1,0:T(8,128)(2,1)S(1)} %collective-permute-done.3), channel_id=1, source_target_pairs={{0,3},{1,0},{2,1},{3,2},{4,7},{5,4},{6,5},{7,6},{8,11},{9,8},{10,9... | collective-permute-start | bytes 921608 | tf_op jit(solution)/shard_map/ppermute | solution.py:69
  85.2 9.9 %collective-permute-start.4 = (bf16[6,8,3200]{2,1,0:T(8,128)(2,1)S(1)}, bf16[6,8,3200]{2,1,0:T(8,128)(2,1)S(1)}, u32[]{:S(2)}, u32[]{:S(2)}) collective-permute-start(bf16[6,8,3200]{2,1,0:T(8,128)(2,1)S(1)} %collective-permute-done.3), channel_id=1, source_target_pairs={{0,1},{1,2},{2,3},{3,0},{4,5},{5,6},{6,7},{7,4},{8,9},{9,10},{10,1... | collective-permute-start | bytes 921608 | tf_op jit(solution)/shard_map/ppermute | solution.py:69
  98.7 15.8 %collective-permute-start.7 = (bf16[128,3200]{1,0:T(8,128)(2,1)}, bf16[128,3200]{1,0:T(8,128)(2,1)}, u32[]{:S(2)}, u32[]{:S(2)}) collective-permute-start(bf16[128,3200]{1,0:T(8,128)(2,1)} %get-tuple-element.8), channel_id=1, source_target_pairs={{0,8},{8,0},{16,24},{24,16},{32,40},{40,32},{48,56},{56,48},{64,72... | collective-permute-start | bytes 2457608 | tf_op jit(solution)/shard_map/ppermute | solution.py:231
  116.8 39.0 %all-to-all-start.3 = ((bf16[32,4,4096]{2,1,0:T(4,128)(2,1)}), bf16[32,4,4096]{2,1,0:T(4,128)(2,1)S(1)}, u32[]{:S(2)}, u32[]{:S(2)}) async-start(bf16[32,4,4096]{2,1,0:T(4,128)(2,1)} %outgoing_blocks.1), calls=%async_computation.3 | async-start | bytes 2097152 | tf_op jit(solution)/shard_map/all_to_all | solution.py:237
  130.4 4.6 %copy-start.5 = (bf16[6,64,2,128]{3,2,1,0:T(2,128)(2,1)S(1)}, bf16[6,64,2,128]{3,2,1,0:T(2,128)(2,1)}, u32[]{:S(2)}) copy-start(bf16[6,64,2,128]{3,2,1,0:T(2,128)(2,1)} %copy-done.4) | copy-start | bytes 589828
  134.7 2.2 %copy-start.3 = (bf16[6,64,2,128]{3,2,1,0:T(2,128)(2,1)S(1)}, bf16[6,64,2,128]{3,2,1,0:T(2,128)(2,1)}, u32[]{:S(2)}) copy-start(bf16[6,64,2,128]{3,2,1,0:T(2,128)(2,1)} %copy-done.2) | copy-start | bytes 589828
